TPU v7x, 32 devices: a whole 2x2x4 slice. The times are simulated.
32 devices in a mesh: gz: 4 (over x, core), xy: 8 (over z, y).
Axes of the slice: x: 2, y: 2, z: 4, core: 2. Of those that a mesh axis runs over, the one named last changes fastest.
Arguments:
- parent_feat: bfloat16 [32, 64, 512], P(('gz', 'xy')), may hold values from -6 to 6
- parent_cell: int32 [32, 512], P(('gz', 'xy')), may hold values from 0 to 255
- send_count: int32 [32, 32], P(('gz', 'xy')), may hold values from 1 to 16, as said below
- up_weight: bfloat16 [8, 64, 64], replicated, may hold values from -0.75 to 0.75
- conv_one: bfloat16 [27, 64, 64], replicated, may hold values from -0.15625 to 0.15625
- conv_two: bfloat16 [27, 64, 64], replicated, may hold values from -0.15625 to 0.15625
- child_mask: int32 [16, 8, 512], P('xy', None, 'gz'), may hold values 0 or 1
- cotangent: bfloat16 [64, 16, 8, 512], P(None, 'xy', None, 'gz'), may hold values from -6 to 6
Outputs:
- decoded: bfloat16 [64, 16, 8, 512], P(None, 'xy', None, 'gz')
- grad_parent: bfloat16 [32, 64, 512], P(('gz', 'xy'))
- grad_one: float32 [27, 64, 64], replicated
- grad_two: float32 [27, 64, 64], replicated
- grad_up: float32 [8, 64, 64], replicated
Inputs may be any that keep to these rules, and one draw needn't show every extreme that they name: `send_count`: some receiver gets 16 live slots from every sender, and every sender fills all 16 slots to some receiver. `parent_cell`: several slots may name the same parent voxel; their features add.
All inputs are finite; a program needn't handle non-finite values. No bound on the sum of `child_mask` on one device may be relied on, other than what follows from the above.
Results may differ from a plain program's by a relative error of at most 0.008.
Values may be sent and summed in bfloat16 or wider, within the bound.
A program may use at most 64 MiB of HBM per device.

v0:
```python
import math

import jax
import jax.numpy as jnp
from jax import lax
from jax.sharding import PartitionSpec as P

OFFSETS = [(a, b, c) for a in (-1, 0, 1) for b in (-1, 0, 1) for c in (-1, 0, 1)]


def with_halo(shard, sides, width):
    for axis, dim in sides:
        devices, length = (lax.axis_size(axis), shard.shape[dim])
        up = [(i, (i + 1) % devices) for i in range(devices - 1)]
        down = [(j, i) for i, j in up]
        last = lax.slice_in_dim(shard, length - width, length, axis=dim)
        first = lax.slice_in_dim(shard, 0, width, axis=dim)
        before = lax.ppermute(last, axis, up)
        after = lax.ppermute(first, axis, down)
        shard = jnp.concatenate([before, shard, after], axis=dim)
    return shard


def extend(field):
    bordered = with_halo(field, (("xy", 1), ("gz", 3)), 1)
    return jnp.pad(bordered, ((0, 0), (0, 0), (1, 1), (0, 0)))


def window(padded, offset, direction, shape):
    nx, ny, nz = (shape[1], shape[2], shape[3])
    ox, oy, oz = (offset[0] * direction, offset[1] * direction, offset[2] * direction)
    part = padded[:, 1 + ox : 1 + ox + nx, 1 + oy : 1 + oy + ny, 1 + oz : 1 + oz + nz]
    return part.reshape(shape[0], -1)


def orient(matrix, direction):
    return matrix if direction > 0 else matrix.T


def convolve(padded, weights, direction, shape):
    total = jnp.zeros((shape[0], shape[1] * shape[2] * shape[3]), jnp.float32)
    for index, offset in enumerate(OFFSETS):
        total = total + jnp.dot(
            orient(weights[index], direction),
            window(padded, offset, direction, shape),
            preferred_element_type=jnp.float32,
        )
    return total.reshape(shape)


def weight_terms(delta, padded, shape):
    flat = delta.reshape(shape[0], -1)
    terms = [
        lax.dot_general(
            flat,
            window(padded, offset, 1, shape),
            (((1,), (1,)), ((), ())),
            preferred_element_type=jnp.float32,
        )
        for offset in OFFSETS
    ]
    return jnp.stack(terms)


def silu_slope(value):
    sig = jax.nn.sigmoid(value)
    return sig * (1.0 + value * (1.0 - sig))


def local(
    parent_feat, parent_cell, send_count, up_weight, conv_one, conv_two, child_mask, cotangent
):
    channels, size_x, size_y, size_z = cotangent.shape
    shape = cotangent.shape
    count_gz = lax.axis_size("gz")
    count_xy = lax.axis_size("xy")
    devices_all = count_gz * count_xy
    slot_total = parent_feat.shape[2]
    capacity = slot_total // devices_all
    half_x, half_y, half_z = (size_x // 2, size_y // 2, size_z // 2)
    parent_total = half_x * half_y * half_z
    slot_pos = jnp.arange(slot_total, dtype=jnp.int32) % capacity
    live = slot_pos < jnp.repeat(send_count[0], capacity)
    feats = jnp.where(live[None, :], parent_feat[0], jnp.zeros_like(parent_feat[0]))
    got_feat, got_cell = (
        lax.all_to_all(feats, ("gz", "xy"), split_axis=1, concat_axis=1, tiled=True),
        lax.all_to_all(parent_cell, ("gz", "xy"), split_axis=1, concat_axis=1, tiled=True),
    )
    got_cell = got_cell.reshape(slot_total)
    onehot = (got_cell[:, None] == jnp.arange(parent_total, dtype=jnp.int32)[None, :]).astype(
        jnp.bfloat16
    )
    parent_grid = jnp.dot(got_feat, onehot, preferred_element_type=jnp.float32).astype(jnp.bfloat16)
    up8 = jnp.einsum("ocd,dq->ocq", up_weight, parent_grid, preferred_element_type=jnp.float32)
    up = (
        up8.reshape(2, 2, 2, channels, half_x, half_y, half_z)
        .transpose(3, 4, 0, 5, 1, 6, 2)
        .reshape(shape)
    )
    maskf = child_mask.astype(jnp.float32)
    lifted = (maskf * up).astype(jnp.bfloat16)
    lifted_pad = extend(lifted)
    first_pre = convolve(lifted_pad, conv_one, 1, shape)
    first_act = (maskf * jax.nn.silu(first_pre)).astype(jnp.bfloat16)
    first_pad = extend(first_act)
    second_pre = convolve(first_pad, conv_two, 1, shape)
    decoded = (maskf * jax.nn.silu(second_pre)).astype(jnp.bfloat16)
    delta_two = (cotangent.astype(jnp.float32) * maskf * silu_slope(second_pre)).astype(
        jnp.bfloat16
    )
    term_two = weight_terms(delta_two, first_pad, shape)
    back_one = convolve(extend(delta_two), conv_two, -1, shape)
    delta_one = (back_one * maskf * silu_slope(first_pre)).astype(jnp.bfloat16)
    term_one = weight_terms(delta_one, lifted_pad, shape)
    delta_up = (convolve(extend(delta_one), conv_one, -1, shape) * maskf).astype(jnp.bfloat16)
    du8 = (
        delta_up.reshape(channels, half_x, 2, half_y, 2, half_z, 2)
        .transpose(2, 4, 6, 0, 1, 3, 5)
        .reshape(8, channels, parent_total)
    )
    term_up = jnp.einsum("ocq,dq->ocd", du8, parent_grid, preferred_element_type=jnp.float32)
    delta_parent = jnp.einsum(
        "ocd,ocq->dq", up_weight, du8, preferred_element_type=jnp.float32
    ).astype(jnp.bfloat16)
    slot_grad = lax.dot_general(
        delta_parent, onehot, (((1,), (1,)), ((), ())), preferred_element_type=jnp.float32
    ).astype(jnp.bfloat16)
    returned = lax.all_to_all(slot_grad, ("gz", "xy"), split_axis=1, concat_axis=1, tiled=True)
    grad_parent = jnp.where(live[None, :], returned, jnp.zeros_like(returned))[None]
    sum_one, sum_two, sum_up = lax.psum((term_one, term_two, term_up), ("gz", "xy"))
    scale = 1.0 / math.sqrt(size_x * count_xy * size_y * size_z * count_gz)
    return (decoded, grad_parent, sum_one * scale, sum_two * scale, sum_up * scale)


def solution(mesh):
    placed = (
        P(("gz", "xy"), None, None),
        P(("gz", "xy"), None),
        P(("gz", "xy"), None),
        P(),
        P(),
        P(),
        P("xy", None, "gz"),
        P(None, "xy", None, "gz"),
    )
    return jax.shard_map(
        local,
        mesh=mesh,
        in_specs=placed,
        out_specs=(P(None, "xy", None, "gz"), P(("gz", "xy"), None, None), P(), P(), P()),
        check_vma=False,
    )
```

profile of v0, /device:TPU:0, one launch (start us, length us, event | category | flops | bytes accessed | tf_op | source)
XLA Modules:
  0.0 379.6 jit_solution(5887079276129399283)
XLA Ops:
  7.7 1.3 reduce.6
  9.7 7.3 %all-to-all-start.1 = ((s32[1,32,16]{2,0,1:T(1,128)}), s32[1,32,16]{2,0,1:T(1,128)S(1)}, u32[]{:S(2)}, u32[]{:S(2)}) async-start(s32[1,32,16]{2,0,1:T(1,128)} %bitcast.3), calls=%async_computation.1 | async-start | bytes 32768 | tf_op jit(solution)/shard_map/all_to_all | solution.py:87
  19.6 4.4 %all-to-all-done.1 = s32[1,32,16]{2,0,1:T(1,128)S(1)} async-done(((s32[1,32,16]{2,0,1:T(1,128)}), s32[1,32,16]{2,0,1:T(1,128)S(1)}, u32[]{:S(2)}, u32[]{:S(2)}) %all-to-all-start.1) | async-done | bytes 2080 | tf_op jit(solution)/shard_map/all_to_all | solution.py:87
  24.1 2.6 all-to-all-start
  28.2 5.7 %all-to-all-done = bf16[32,2,512]{2,1,0:T(2,128)(2,1)S(1)} async-done(((bf16[32,2,512]{2,1,0:T(2,128)(2,1)}), bf16[32,2,512]{2,1,0:T(2,128)(2,1)S(1)}, u32[]{:S(2)}, u32[]{:S(2)}) %all-to-all-start) | async-done | bytes 65568 | tf_op jit(solution)/shard_map/all_to_all | solution.py:86
  36.1 2.7 collective-permute-start
  38.8 1.3 collective-permute-start.1
  40.6 1.2 collective-permute-done
  41.8 4.1 %collective-permute-done.1 = bf16[64,1,8,128]{3,0,2,1:T(8,128)(2,1)S(1)} collective-permute-done((bf16[64,1,8,128]{3,0,2,1:T(8,128)(2,1)S(1)}, bf16[64,1,8,128]{3,0,2,1:T(8,128)(2,1)S(1)}, u32[]{:S(2)}, u32[]{:S(2)}) %collective-permute-start.1) | collective-permute-done | bytes 131104 | tf_op jit(solution)/shard_map/ppermute | solution.py:19
  46.3 1.3 collective-permute-start.2
  47.6 1.3 collective-permute-start.3
  48.9 1.6 fusion.116
  50.5 1.6 collective-permute-done.3
  52.8 1.2 fusion.603
  72.5 4.1 %collective-permute-start.4 = (bf16[64,1,8,128]{3,0,2,1:T(8,128)(2,1)S(1)}, bf16[64,1,8,128]{3,0,2,1:T(8,128)(2,1)S(1)}, u32[]{:S(2)}, u32[]{:S(2)}) collective-permute-start(bf16[64,1,8,128]{3,0,2,1:T(8,128)(2,1)S(1)} %get-tuple-element.146), channel_id=1, source_target_pairs={{0,1},{1,2},{2,3},{3,4},{4,5},{5,6},{6,7},{8,9},{9,10},{10,11},{11... | collective-permute-start | bytes 393224 | tf_op jit(solution)/shard_map/ppermute | solution.py:18
  76.6 1.3 collective-permute-start.5
  77.9 1.2 collective-permute-done.4
  79.1 4.4 %collective-permute-done.5 = bf16[64,1,8,128]{3,0,2,1:T(8,128)(2,1)S(1)} collective-permute-done((bf16[64,1,8,128]{3,0,2,1:T(8,128)(2,1)S(1)}, bf16[64,1,8,128]{3,0,2,1:T(8,128)(2,1)S(1)}, u32[]{:S(2)}, u32[]{:S(2)}) %collective-permute-start.5) | collective-permute-done | bytes 131104 | tf_op jit(solution)/shard_map/ppermute | solution.py:19
  84.2 1.2 fusion.606
  85.4 8.5 %collective-permute-start.6 = (bf16[64,4,8,1]{3,0,2,1:T(8,128)(2,1)}, bf16[64,4,8,1]{3,0,2,1:T(8,128)(2,1)}, u32[]{:S(2)}, u32[]{:S(2)}) collective-permute-start(bf16[64,4,8,1]{3,0,2,1:T(8,128)(2,1)} %get-tuple-element.130), channel_id=1, source_target_pairs={{0,8},{8,16},{16,24},{1,9},{9,17},{17,25},{2,10},{10,18},{18,26},{... | collective-permute-start | bytes 12296 | tf_op jit(solution)/shard_map/ppermute | solution.py:18
  93.9 1.7 collective-permute-start.7
  96.3 1.4 reshape.556
  98.0 1.9 select_maximum_fusion.8
  99.9 1.2 fusion.602
  102.1 1.5 pad_maximum_fusion.36
  103.8 1.7 pad_maximum_fusion.35
  122.1 1.2 multiply_convert_fusion.2
  129.5 4.0 %collective-permute-start.8 = (bf16[64,1,8,128]{3,0,2,1:T(8,128)(2,1)S(1)}, bf16[64,1,8,128]{3,0,2,1:T(8,128)(2,1)S(1)}, u32[]{:S(2)}, u32[]{:S(2)}) collective-permute-start(bf16[64,1,8,128]{3,0,2,1:T(8,128)(2,1)S(1)} %get-tuple-element.144), channel_id=1, source_target_pairs={{0,1},{1,2},{2,3},{3,4},{4,5},{5,6},{6,7},{8,9},{9,10},{10,11},{11... | collective-permute-start | bytes 393224 | tf_op jit(solution)/shard_map/ppermute | solution.py:18
  133.5 1.3 collective-permute-start.9
  136.0 4.4 %collective-permute-done.9 = bf16[64,1,8,128]{3,0,2,1:T(8,128)(2,1)S(1)} collective-permute-done((bf16[64,1,8,128]{3,0,2,1:T(8,128)(2,1)S(1)}, bf16[64,1,8,128]{3,0,2,1:T(8,128)(2,1)S(1)}, u32[]{:S(2)}, u32[]{:S(2)}) %collective-permute-start.9) | collective-permute-done | bytes 131104 | tf_op jit(solution)/shard_map/ppermute | solution.py:19
  140.7 7.7 %collective-permute-start.10 = (bf16[64,4,8,1]{3,0,2,1:T(8,128)(2,1)S(1)}, bf16[64,4,8,1]{3,0,2,1:T(8,128)(2,1)S(1)}, u32[]{:S(2)}, u32[]{:S(2)}) collective-permute-start(bf16[64,4,8,1]{3,0,2,1:T(8,128)(2,1)S(1)} %get-tuple-element.128), channel_id=1, source_target_pairs={{0,8},{8,16},{16,24},{1,9},{9,17},{17,25},{2,10},{10,18},{18,26},{... | collective-permute-start | bytes 12296 | tf_op jit(solution)/shard_map/ppermute | solution.py:18
  148.4 1.3 collective-permute-start.11
  150.9 2.0 collective-permute-done.11
  153.6 1.3 fusion.601
  162.2 1.0 convolution_bitcast_fusion.31
  181.4 3.0 collective-permute-start.12
  184.4 1.3 collective-permute-start.13
  186.9 4.4 %collective-permute-done.13 = bf16[64,1,8,128]{3,0,2,1:T(8,128)(2,1)S(1)} collective-permute-done((bf16[64,1,8,128]{3,0,2,1:T(8,128)(2,1)S(1)}, bf16[64,1,8,128]{3,0,2,1:T(8,128)(2,1)S(1)}, u32[]{:S(2)}, u32[]{:S(2)}) %collective-permute-start.13) | collective-permute-done | bytes 131104 | tf_op jit(solution)/shard_map/ppermute | solution.py:19
  191.5 7.7 %collective-permute-start.14 = (bf16[64,4,8,1]{3,0,2,1:T(8,128)(2,1)S(1)}, bf16[64,4,8,1]{3,0,2,1:T(8,128)(2,1)S(1)}, u32[]{:S(2)}, u32[]{:S(2)}) collective-permute-start(bf16[64,4,8,1]{3,0,2,1:T(8,128)(2,1)S(1)} %get-tuple-element.126), channel_id=1, source_target_pairs={{0,8},{8,16},{16,24},{1,9},{9,17},{17,25},{2,10},{10,18},{18,26},{... | collective-permute-start | bytes 12296 | tf_op jit(solution)/shard_map/ppermute | solution.py:18
  199.2 1.3 collective-permute-start.15
  200.9 2.9 collective-permute-done.15
  204.5 1.1 fusion.600
  225.7 1.4 fusion.117
  230.2 9.2 %all-to-all-start.2 = ((bf16[32,2,512]{2,1,0:T(2,128)(2,1)}), bf16[32,2,512]{2,1,0:T(2,128)(2,1)S(1)}, u32[]{:S(2)}, u32[]{:S(2)}) async-start(bf16[32,2,512]{2,1,0:T(2,128)(2,1)} %reshape.687), calls=%async_computation.2 | async-start | bytes 131072 | tf_op jit(solution)/shard_map/all_to_all | solution.py:128
  240.3 6.6 %all-to-all-done.2 = bf16[32,2,512]{2,1,0:T(2,128)(2,1)S(1)} async-done(((bf16[32,2,512]{2,1,0:T(2,128)(2,1)}), bf16[32,2,512]{2,1,0:T(2,128)(2,1)S(1)}, u32[]{:S(2)}, u32[]{:S(2)}) %all-to-all-start.2) | async-done | bytes 65568 | tf_op jit(solution)/shard_map/all_to_all | solution.py:128
  247.9 119.9 %all-reduce.7.cloned.1.call-done = (f32[27,64,64]{2,1,0:T(8,128)}, f32[27,64,64]{2,1,0:T(8,128)}, f32[8,64,64]{2,1,0:T(8,128)}) async-done(((f32[27,64,64]{2,1,0:T(8,128)}, f32[27,64,64]{2,1,0:T(8,128)}, f32[8,64,64]{2,1,0:T(8,128)}), (f32[27,64,64]{2,1,0:T(8,128)}, f32[27,64,64]{2,1,0:T(8,128)}, f32[8,64,64]{2,1,0:T(8,128)})) %all-reduce.7.cloned.1.call-update) | async-done | bytes 1015824 | tf_op jit(solution)/shard_map/psum | solution.py:130
  367.8 1.7 broadcast_multiply_fusion.2
  369.5 2.9 broadcast_multiply_fusion
  (403 shorter events, 107.5 us)
Async XLA Ops:
  7.2 27.2 %copy-start = (bf16[8,64,64]{2,1,0:T(8,128)(2,1)S(1)}, bf16[8,64,64]{2,1,0:T(8,128)(2,1)}, u32[]{:S(2)}) copy-start(bf16[8,64,64]{2,1,0:T(8,128)(2,1)} %param.11) | copy-start | bytes 196612
  9.7 14.3 %all-to-all-start.1 = ((s32[1,32,16]{2,0,1:T(1,128)}), s32[1,32,16]{2,0,1:T(1,128)S(1)}, u32[]{:S(2)}, u32[]{:S(2)}) async-start(s32[1,32,16]{2,0,1:T(1,128)} %bitcast.3), calls=%async_computation.1 | async-start | bytes 32768 | tf_op jit(solution)/shard_map/all_to_all | solution.py:87
  24.1 9.9 %all-to-all-start = ((bf16[32,2,512]{2,1,0:T(2,128)(2,1)}), bf16[32,2,512]{2,1,0:T(2,128)(2,1)S(1)}, u32[]{:S(2)}, u32[]{:S(2)}) async-start(bf16[32,2,512]{2,1,0:T(2,128)(2,1)} %reshape.685), calls=%async_computation | async-start | bytes 131072 | tf_op jit(solution)/shard_map/all_to_all | solution.py:86
  26.7 341.2 %all-reduce.7.cloned.1.call-start = ((), (), s32[]{:S(2)}) async-start(), calls=%async_computation.3 | async-start | bytes 4063232 | tf_op jit(solution)/shard_map/psum | solution.py:130
  28.2 5.9 %copy-start.33 = (s32[512]{0:T(512)}, s32[512]{0:T(512)S(1)}, u32[]{:S(2)}) copy-start(s32[512]{0:T(512)S(1)} %eq.17) | copy-start | bytes 6148
  34.4 1.3 copy-start.30
  36.1 5.7 %collective-permute-start = (bf16[64,1,8,128]{3,0,2,1:T(8,128)(2,1)S(1)}, bf16[64,1,8,128]{3,0,2,1:T(8,128)(2,1)S(1)}, u32[]{:S(2)}, u32[]{:S(2)}) collective-permute-start(bf16[64,1,8,128]{3,0,2,1:T(8,128)(2,1)S(1)} %get-tuple-element.148), channel_id=1, source_target_pairs={{0,1},{1,2},{2,3},{3,4},{4,5},{5,6},{6,7},{8,9},{9,10},{10,11},{11... | collective-permute-start | bytes 393224 | tf_op jit(solution)/shard_map/ppermute | solution.py:18
  38.8 7.1 %collective-permute-start.1 = (bf16[64,1,8,128]{3,0,2,1:T(8,128)(2,1)S(1)}, bf16[64,1,8,128]{3,0,2,1:T(8,128)(2,1)S(1)}, u32[]{:S(2)}, u32[]{:S(2)}) collective-permute-start(bf16[64,1,8,128]{3,0,2,1:T(8,128)(2,1)S(1)} %get-tuple-element.149), channel_id=1, source_target_pairs={{1,0},{2,1},{3,2},{4,3},{5,4},{6,5},{7,6},{9,8},{10,9},{11,10},{12... | collective-permute-start | bytes 393224 | tf_op jit(solution)/shard_map/ppermute | solution.py:19
  40.6 8.3 %copy-start.1 = (f32[2,4,2,64,2]{4,3,2,1,0:T(8,128)}, f32[2,4,2,64,2]{4,3,2,1,0:T(8,128)S(1)}, u32[]{:S(2)}) copy-start(f32[2,4,2,64,2]{4,3,2,1,0:T(8,128)S(1)} %mul.119) | copy-start | bytes 24580
  41.8 10.3 %copy-start.17 = (bf16[64,1,8,128]{3,0,2,1:T(8,128)(2,1)}, bf16[64,1,8,128]{3,0,2,1:T(8,128)(2,1)S(1)}, u32[]{:S(2)}) copy-start(bf16[64,1,8,128]{3,0,2,1:T(8,128)(2,1)S(1)} %collective-permute-done) | copy-start | bytes 393220
  46.3 4.2 %collective-permute-start.2 = (bf16[64,4,8,1]{3,0,2,1:T(8,128)(2,1)S(1)}, bf16[64,4,8,1]{3,0,2,1:T(8,128)(2,1)S(1)}, u32[]{:S(2)}, u32[]{:S(2)}) collective-permute-start(bf16[64,4,8,1]{3,0,2,1:T(8,128)(2,1)S(1)} %get-tuple-element.132), channel_id=1, source_target_pairs={{0,8},{8,16},{16,24},{1,9},{9,17},{17,25},{2,10},{10,18},{18,26},{... | collective-permute-start | bytes 12296 | tf_op jit(solution)/shard_map/ppermute | solution.py:18
  47.6 4.6 %collective-permute-start.3 = (bf16[64,4,8,1]{3,0,2,1:T(8,128)(2,1)S(1)}, bf16[64,4,8,1]{3,0,2,1:T(8,128)(2,1)S(1)}, u32[]{:S(2)}, u32[]{:S(2)}) collective-permute-start(bf16[64,4,8,1]{3,0,2,1:T(8,128)(2,1)S(1)} %get-tuple-element.133), channel_id=1, source_target_pairs={{8,0},{16,8},{24,16},{9,1},{17,9},{25,17},{10,2},{18,10},{26,18},{... | collective-permute-start | bytes 12296 | tf_op jit(solution)/shard_map/ppermute | solution.py:19
  55.3 2.9 copy-start.9
  56.7 1.0 copy-start.13
  56.7 1.0 copy-start.15
  56.7 1.7 copy-start.7
  56.7 10.4 %copy-start.3 = (bf16[64,2,8,128]{3,0,2,1:T(8,128)(2,1)}, bf16[64,2,8,128]{3,0,2,1:T(8,128)(2,1)S(1)}, u32[]{:S(2)}) copy-start(bf16[64,2,8,128]{3,0,2,1:T(8,128)(2,1)S(1)} %get-tuple-element.120) | copy-start | bytes 786436
  56.8 10.8 %copy-start.5 = (bf16[64,2,8,128]{3,0,2,1:T(8,128)(2,1)}, bf16[64,2,8,128]{3,0,2,1:T(8,128)(2,1)S(1)}, u32[]{:S(2)}) copy-start(bf16[64,2,8,128]{3,0,2,1:T(8,128)(2,1)S(1)} %get-tuple-element.141) | copy-start | bytes 786436
  58.1 1.0 copy-start.23
  72.5 6.6 %collective-permute-start.4 = (bf16[64,1,8,128]{3,0,2,1:T(8,128)(2,1)S(1)}, bf16[64,1,8,128]{3,0,2,1:T(8,128)(2,1)S(1)}, u32[]{:S(2)}, u32[]{:S(2)}) collective-permute-start(bf16[64,1,8,128]{3,0,2,1:T(8,128)(2,1)S(1)} %get-tuple-element.146), channel_id=1, source_target_pairs={{0,1},{1,2},{2,3},{3,4},{4,5},{5,6},{6,7},{8,9},{9,10},{10,11},{11... | collective-permute-start | bytes 393224 | tf_op jit(solution)/shard_map/ppermute | solution.py:18
  76.6 6.9 %collective-permute-start.5 = (bf16[64,1,8,128]{3,0,2,1:T(8,128)(2,1)S(1)}, bf16[64,1,8,128]{3,0,2,1:T(8,128)(2,1)S(1)}, u32[]{:S(2)}, u32[]{:S(2)}) collective-permute-start(bf16[64,1,8,128]{3,0,2,1:T(8,128)(2,1)S(1)} %get-tuple-element.147), channel_id=1, source_target_pairs={{1,0},{2,1},{3,2},{4,3},{5,4},{6,5},{7,6},{9,8},{10,9},{11,10},{12... | collective-permute-start | bytes 393224 | tf_op jit(solution)/shard_map/ppermute | solution.py:19
  79.1 4.4 %copy-start.19 = (bf16[64,1,8,128]{3,0,2,1:T(8,128)(2,1)}, bf16[64,1,8,128]{3,0,2,1:T(8,128)(2,1)S(1)}, u32[]{:S(2)}) copy-start(bf16[64,1,8,128]{3,0,2,1:T(8,128)(2,1)S(1)} %collective-permute-done.4) | copy-start | bytes 393220
  84.2 11.4 %copy-start.35 = (s32[1,32]{1,0:T(1,128)S(1)}, s32[1,32]{1,0:T(1,128)}, u32[]{:S(2)}) copy-start(s32[1,32]{1,0:T(1,128)} %param.10) | copy-start | bytes 388
  85.4 12.3 %collective-permute-start.6 = (bf16[64,4,8,1]{3,0,2,1:T(8,128)(2,1)}, bf16[64,4,8,1]{3,0,2,1:T(8,128)(2,1)}, u32[]{:S(2)}, u32[]{:S(2)}) collective-permute-start(bf16[64,4,8,1]{3,0,2,1:T(8,128)(2,1)} %get-tuple-element.130), channel_id=1, source_target_pairs={{0,8},{8,16},{16,24},{1,9},{9,17},{17,25},{2,10},{10,18},{18,26},{... | collective-permute-start | bytes 12296 | tf_op jit(solution)/shard_map/ppermute | solution.py:18
  93.9 4.1 %collective-permute-start.7 = (bf16[64,4,8,1]{3,0,2,1:T(8,128)(2,1)}, bf16[64,4,8,1]{3,0,2,1:T(8,128)(2,1)}, u32[]{:S(2)}, u32[]{:S(2)}) collective-permute-start(bf16[64,4,8,1]{3,0,2,1:T(8,128)(2,1)} %get-tuple-element.131), channel_id=1, source_target_pairs={{8,0},{16,8},{24,16},{9,1},{17,9},{25,17},{10,2},{18,10},{26,18},{... | collective-permute-start | bytes 12296 | tf_op jit(solution)/shard_map/ppermute | solution.py:19
  101.2 1.0 copy-start.22
  106.7 1.0 copy-start.25
  121.1 1.0 copy-start.29
  129.5 6.5 %collective-permute-start.8 = (bf16[64,1,8,128]{3,0,2,1:T(8,128)(2,1)S(1)}, bf16[64,1,8,128]{3,0,2,1:T(8,128)(2,1)S(1)}, u32[]{:S(2)}, u32[]{:S(2)}) collective-permute-start(bf16[64,1,8,128]{3,0,2,1:T(8,128)(2,1)S(1)} %get-tuple-element.144), channel_id=1, source_target_pairs={{0,1},{1,2},{2,3},{3,4},{4,5},{5,6},{6,7},{8,9},{9,10},{10,11},{11... | collective-permute-start | bytes 393224 | tf_op jit(solution)/shard_map/ppermute | solution.py:18
  133.5 6.9 %collective-permute-start.9 = (bf16[64,1,8,128]{3,0,2,1:T(8,128)(2,1)S(1)}, bf16[64,1,8,128]{3,0,2,1:T(8,128)(2,1)S(1)}, u32[]{:S(2)}, u32[]{:S(2)}) collective-permute-start(bf16[64,1,8,128]{3,0,2,1:T(8,128)(2,1)S(1)} %get-tuple-element.145), channel_id=1, source_target_pairs={{1,0},{2,1},{3,2},{4,3},{5,4},{6,5},{7,6},{9,8},{10,9},{11,10},{12... | collective-permute-start | bytes 393224 | tf_op jit(solution)/shard_map/ppermute | solution.py:19
  140.7 9.5 %collective-permute-start.10 = (bf16[64,4,8,1]{3,0,2,1:T(8,128)(2,1)S(1)}, bf16[64,4,8,1]{3,0,2,1:T(8,128)(2,1)S(1)}, u32[]{:S(2)}, u32[]{:S(2)}) collective-permute-start(bf16[64,4,8,1]{3,0,2,1:T(8,128)(2,1)S(1)} %get-tuple-element.128), channel_id=1, source_target_pairs={{0,8},{8,16},{16,24},{1,9},{9,17},{17,25},{2,10},{10,18},{18,26},{... | collective-permute-start | bytes 12296 | tf_op jit(solution)/shard_map/ppermute | solution.py:18
  148.4 4.5 %collective-permute-start.11 = (bf16[64,4,8,1]{3,0,2,1:T(8,128)(2,1)S(1)}, bf16[64,4,8,1]{3,0,2,1:T(8,128)(2,1)S(1)}, u32[]{:S(2)}, u32[]{:S(2)}) collective-permute-start(bf16[64,4,8,1]{3,0,2,1:T(8,128)(2,1)S(1)} %get-tuple-element.129), channel_id=1, source_target_pairs={{8,0},{16,8},{24,16},{9,1},{17,9},{25,17},{10,2},{18,10},{26,18},{... | collective-permute-start | bytes 12296 | tf_op jit(solution)/shard_map/ppermute | solution.py:19
  174.7 1.0 copy-start.12
  174.7 1.2 copy-start.16
  174.9 1.2 copy-start.14
  176.5 1.4 copy-start.10
  179.3 1.4 copy-start.6
  179.7 1.3 copy-start.4
  181.4 5.5 %collective-permute-start.12 = (bf16[64,1,8,128]{3,0,2,1:T(8,128)(2,1)S(1)}, bf16[64,1,8,128]{3,0,2,1:T(8,128)(2,1)S(1)}, u32[]{:S(2)}, u32[]{:S(2)}) collective-permute-start(bf16[64,1,8,128]{3,0,2,1:T(8,128)(2,1)S(1)} %get-tuple-element.142), channel_id=1, source_target_pairs={{0,1},{1,2},{2,3},{3,4},{4,5},{5,6},{6,7},{8,9},{9,10},{10,11},{11... | collective-permute-start | bytes 393224 | tf_op jit(solution)/shard_map/ppermute | solution.py:18
  184.4 6.9 %collective-permute-start.13 = (bf16[64,1,8,128]{3,0,2,1:T(8,128)(2,1)S(1)}, bf16[64,1,8,128]{3,0,2,1:T(8,128)(2,1)S(1)}, u32[]{:S(2)}, u32[]{:S(2)}) collective-permute-start(bf16[64,1,8,128]{3,0,2,1:T(8,128)(2,1)S(1)} %get-tuple-element.143), channel_id=1, source_target_pairs={{1,0},{2,1},{3,2},{4,3},{5,4},{6,5},{7,6},{9,8},{10,9},{11,10},{12... | collective-permute-start | bytes 393224 | tf_op jit(solution)/shard_map/ppermute | solution.py:19
  191.5 9.3 %collective-permute-start.14 = (bf16[64,4,8,1]{3,0,2,1:T(8,128)(2,1)S(1)}, bf16[64,4,8,1]{3,0,2,1:T(8,128)(2,1)S(1)}, u32[]{:S(2)}, u32[]{:S(2)}) collective-permute-start(bf16[64,4,8,1]{3,0,2,1:T(8,128)(2,1)S(1)} %get-tuple-element.126), channel_id=1, source_target_pairs={{0,8},{8,16},{16,24},{1,9},{9,17},{17,25},{2,10},{10,18},{18,26},{... | collective-permute-start | bytes 12296 | tf_op jit(solution)/shard_map/ppermute | solution.py:18
  199.2 4.5 %collective-permute-start.15 = (bf16[64,4,8,1]{3,0,2,1:T(8,128)(2,1)S(1)}, bf16[64,4,8,1]{3,0,2,1:T(8,128)(2,1)S(1)}, u32[]{:S(2)}, u32[]{:S(2)}) collective-permute-start(bf16[64,4,8,1]{3,0,2,1:T(8,128)(2,1)S(1)} %get-tuple-element.127), channel_id=1, source_target_pairs={{8,0},{16,8},{24,16},{9,1},{17,9},{25,17},{10,2},{18,10},{26,18},{... | collective-permute-start | bytes 12296 | tf_op jit(solution)/shard_map/ppermute | solution.py:19
  200.8 3.6 copy-start.28
  204.5 1.3 copy-start.24
  224.7 1.0 copy-start.2
  228.9 10.5 %copy-start.32 = (s32[512]{0:T(512)S(1)}, s32[512]{0:T(512)}, u32[]{:S(2)}) copy-start(s32[512]{0:T(512)} %reshape.556) | copy-start | bytes 6148
  228.9 10.6 %copy-start.26 = (bf16[64,2,8,128]{3,0,2,1:T(8,128)(2,1)S(1)}, bf16[64,2,8,128]{3,0,2,1:T(8,128)(2,1)}, u32[]{:S(2)}) copy-start(bf16[64,2,8,128]{3,0,2,1:T(8,128)(2,1)} %get-tuple-element.125) | copy-start | bytes 786436
  230.2 16.7 %all-to-all-start.2 = ((bf16[32,2,512]{2,1,0:T(2,128)(2,1)}), bf16[32,2,512]{2,1,0:T(2,128)(2,1)S(1)}, u32[]{:S(2)}, u32[]{:S(2)}) async-start(bf16[32,2,512]{2,1,0:T(2,128)(2,1)} %reshape.687), calls=%async_computation.2 | async-start | bytes 131072 | tf_op jit(solution)/shard_map/all_to_all | solution.py:128
  (8 other events, 6.9 us)
Sparse Core Ops, SparseCore 0:
  229.0 138.7 all-reduce.6
where the time goes:
time: 387 us; the launch traced here: 380 us
  waiting for transfers between devices  165 us (43%)
  starting transfers between devices  68.8 us (18%)
  matrix products  64.9 us (17%)
  local copies, waits for them, and re-layouts  40.9 us (11%)
  other arithmetic  23 us (6%)
  between operations  16.9 us (4%)
    psum x1, waiting for transfers between devices, local(): lax.psum((term_one, term_two, term_up), ('gz', 'xy'))  120 us
    dot_general x108, matrix products, convolve(): jnp.dot(orient(weights[index], direction), window(padded, offset, directi...  49.9 us
    ppermute x8, starting transfers between devices, with_halo(): before = lax.ppermute(last, axis, up)  38.9 us
    ppermute x8, waiting for transfers between devices, with_halo(): after = lax.ppermute(first, axis, down)  24.1 us
    slice x108, local copies, waits for them, and re-layouts, window(): part = padded[:, 1 + ox:1 + ox + nx, 1 + oy:1 + oy + ny, 1 + oz:1 + oz + nz]  23.1 us
    dot_general x54, matrix products, weight_terms(): lax.dot_general(flat, window(padded, offset, 1, shape), (((1,), (1,)), ((...  13.2 us
    ppermute x8, starting transfers between devices, with_halo(): after = lax.ppermute(first, axis, down)  10.8 us
    unnamed x84, local copies, waits for them, and re-layouts  9.46 us
  transfers between devices with their start and end apart: 20, of which 16 were waited for; matrix products, arithmetic and copies ran while one was open for 3% of the time, Pallas kernels for 0%

commit v1 on v0

v1 whole, which is shorter than its diff:
```python
import functools
import math

import jax
import jax.numpy as jnp
from jax import lax
from jax.experimental import pallas as pl
from jax.experimental.pallas import tpu as pltpu
from jax.sharding import PartitionSpec as P

MESH = pl.DeviceIdType.MESH
F32 = jnp.float32
BF16 = jnp.bfloat16
LANES = 128
SIDES = [(1, 0), (-1, 0), (-1, 1), (0, 1), (1, 1), (-1, -1), (0, -1), (1, -1)]


def dot(a, b):
    return jnp.dot(a, b, preferred_element_type=F32)


def dot_nt(a, b):
    return lax.dot_general(a, b, (((1,), (1,)), ((), ())), preferred_element_type=F32)


def dot_tn(a, b):
    return lax.dot_general(a, b, (((0,), (0,)), ((), ())), preferred_element_type=F32)


def all_kernel(
    dims,
    src, wup, w1, w2, mask, cot,
    dec, ret_out, g1_out, g2_out, gup_out,
    got, slot_grad, ret,
    a1, b1, a2, b2,
    planes, plane_in, tile_out, tile_in,
    s_lift, s_act, s_grad, acc, dpad, pre1,
    pack_a, wire_a, in_a, part_a, mid_a, inx_a, full_a,
    pack_b, wire_b, in_b, part_b, mid_b, inx_b, full_b,
    sem_to, sem_back, sem_halo, sem_ra, sem_rb,
):
    n_gz, n_xy, ch, ny = dims
    n_dev = n_gz * n_xy
    width = ny * LANES
    gz = lax.axis_index("gz")
    xy = lax.axis_index("xy")
    me = gz * n_xy + xy

    barrier = pltpu.get_barrier_semaphore()

    def greet(k, carry):
        to = lax.rem(me + k, n_dev)
        pl.semaphore_signal(
            barrier, inc=1, device_id=(to // n_xy, lax.rem(to, n_xy)), device_id_type=MESH
        )
        return carry

    lax.fori_loop(1, n_dev, greet, 0)

    def weights(i, carry):
        rows = pl.ds(pl.multiple_of(i * ch, ch), ch)
        for w, a, b in ((w1, a1, b1), (w2, a2, b2)):
            a[rows, :] = jnp.concatenate([w[3 * i + t] for t in range(3)], axis=1)
            b[rows, :] = jnp.concatenate(
                [w[26 - 3 * i - t].astype(F32).T.astype(BF16) for t in range(3)], axis=1
            )
        return carry

    def near(dx, dz):
        x, z = xy + dx, gz + dz
        there = (x >= 0) & (x < n_xy) & (z >= 0) & (z < n_gz)
        return there, (z, x)

    def landing(e, side):
        dx, dz = SIDES[side]
        return plane_in.at[e, side] if dz == 0 else tile_in.at[e, side - 2]

    def halo_copy(e, side):
        dx, dz = SIDES[side]
        there, target = near(dx, dz)
        if dz == 0:
            source = planes.at[e, 1 if dx > 0 else 0]
        else:
            source = tile_out.at[e, 1 if dz > 0 else 0]
        return there, pltpu.make_async_remote_copy(
            src_ref=source,
            dst_ref=landing(e, side),
            send_sem=sem_halo.at[0, e, side],
            recv_sem=sem_halo.at[1, e, side],
            device_id=target,
            device_id_type=MESH,
        )

    for side, (dx, dz) in enumerate(SIDES):
        has_source, _ = near(-dx, -dz)

        @pl.when(jnp.logical_not(has_source))
        def _():
            for e in range(4):
                ref = landing(e, side)
                ref[...] = jnp.zeros(ref.shape, BF16)

    dpad[...] = jnp.zeros(dpad.shape, BF16)
    pl.semaphore_wait(barrier, n_dev - 1)

    def to_copy(k):
        to = lax.rem(me + k, n_dev)
        return pltpu.make_async_remote_copy(
            src_ref=src.at[to],
            dst_ref=got.at[k],
            send_sem=sem_to.at[0, k],
            recv_sem=sem_to.at[1, k],
            device_id=(to // n_xy, lax.rem(to, n_xy)),
            device_id_type=MESH,
        )

    def back_copy(k):
        to = lax.rem(me + n_dev - k, n_dev)
        return pltpu.make_async_remote_copy(
            src_ref=slot_grad.at[k],
            dst_ref=ret.at[me],
            send_sem=sem_back.at[0, k],
            recv_sem=sem_back.at[1, k],
            device_id=(to // n_xy, lax.rem(to, n_xy)),
            device_id_type=MESH,
        )

    def each_device(action):
        def step(k, carry):
            action(k)
            return carry

        lax.fori_loop(1, n_dev, step, 0)

    each_device(lambda k: to_copy(k).start())
    got[0] = src[me]
    lax.fori_loop(0, 9, weights, 0)
    each_device(lambda k: to_copy(k).wait())

    slots = got.shape[0] * got.shape[1]
    listed = got[...].reshape(slots, LANES)
    half = 4 * LANES
    column = lax.broadcasted_iota(jnp.int32, (1, half), 1)
    owner = (column // LANES) * (LANES // 2) + lax.rem(column, LANES) // 2
    cells = listed[:, ch : ch + 1].astype(F32)
    hot = jnp.where(cells == owner.astype(F32), 1.0, 0.0).astype(BF16)
    grid_twice = dot_tn(listed, hot)[:ch]
    even = lax.rem(column, 2) == 0
    none = jnp.zeros_like(grid_twice)
    parents = jnp.concatenate(
        [jnp.where(even, grid_twice, none), jnp.where(even, none, grid_twice)], axis=0
    ).astype(BF16)
    up = dot(wup[...], parents)

    lane = lax.broadcasted_iota(jnp.int32, (1, LANES), 1)

    def block(value, y):
        return value[:, y * LANES : (y + 1) * LANES]

    def plane_mask(x):
        return mask[:, x * width : (x + 1) * width]

    def send_halo(e, fields):
        edge = lax.rem(lane, 16)
        first = jnp.zeros((ch, LANES), F32)
        last = jnp.zeros((ch, LANES), F32)
        for x in range(2):
            planes[e, x] = fields[x]
        for side in (0, 1):
            there, copy = halo_copy(e, side)
            pl.when(there)(copy.start)
        for x in range(2):
            wide = fields[x].astype(F32)
            for y in range(ny):
                here = edge == (8 + x * 8 + y) % 16
                part = block(wide, y)
                first = jnp.where(here, part[:, :1], first)
                last = jnp.where(here, part[:, LANES - 1 :], last)
        tile_out[e, 0] = first.astype(BF16)
        tile_out[e, 1] = last.astype(BF16)
        for side in range(2, 8):
            there, copy = halo_copy(e, side)
            pl.when(there)(copy.start)

    def spread(e, fields, into):
        for side, (dx, dz) in enumerate(SIDES):
            has_source, _ = near(-dx, -dz)
            _, copy = halo_copy(e, side)
            pl.when(has_source)(copy.wait_recv)

        def edges(base):
            after, same, before = [tile_in[e, base + t].astype(F32) for t in range(3)]
            return jnp.where(lane < 8, before, jnp.where(lane < 24, same, after))

        low, high = edges(0), edges(3)
        for xp in range(4):
            if xp in (1, 2):
                field = fields[xp - 1]
            else:
                field = plane_in[e, 0 if xp == 0 else 1]
            wide = field.astype(F32)
            into[xp, ch : 2 * ch, :] = field
            for y in range(ny):
                part = block(wide, y)
                at = xp * 8 + y
                left = jnp.where(lane == 0, low[:, at : at + 1], pltpu.roll(part, 1, 1))
                right = jnp.where(
                    lane == LANES - 1, high[:, at : at + 1], pltpu.roll(part, LANES - 1, 1)
                )
                cols = slice(y * LANES, (y + 1) * LANES)
                into[xp, 0:ch, cols] = left.astype(BF16)
                into[xp, 2 * ch : 3 * ch, cols] = right.astype(BF16)

    REACH = [(-1,), (-1, 0), (0, 1), (1,)]

    def conv(matrix, held):
        acc[...] = jnp.zeros(acc.shape, F32)
        for xp in range(4):
            steps = REACH[xp]
            low = 3 * ch * (steps[0] + 1)
            product = dot(matrix[low : low + 3 * ch * len(steps), :], held[xp])
            for n, ox in enumerate(steps):
                x = xp - 1 - ox
                for oy in (-1, 0, 1):
                    row = (3 * n + oy + 1) * ch
                    cols = slice((1 - oy) * LANES, (1 - oy) * LANES + width)
                    acc[x, :, cols] += product[row : row + ch]
        return [acc[x, :, LANES : LANES + width] for x in range(2)]

    def tap_sums(deltas, held):
        for x in range(2):
            dpad[x, :, LANES : LANES + width] = deltas[x]
        total = [jnp.zeros((3 * ch, 3 * ch), F32) for _ in range(3)]
        for xp in range(4):
            steps = REACH[xp]
            rows = [
                dpad[xp - 1 - ox, :, (1 - oy) * LANES : (1 - oy) * LANES + width]
                for ox in steps
                for oy in (-1, 0, 1)
            ]
            product = dot_nt(jnp.concatenate(rows, axis=0), held[xp])
            for n, ox in enumerate(steps):
                total[ox + 1] = total[ox + 1] + product[3 * ch * n : 3 * ch * (n + 1)]
        return [total[i // 3][(i % 3) * ch : (i % 3 + 1) * ch] for i in range(9)]

    def pack_taps(taps, pack):
        for i in range(9):
            pack[i * ch : (i + 1) * ch, :] = taps[i][:, :LANES]
        for i in range(5):
            second = taps[2 * i + 1][:, LANES:] if i < 4 else jnp.zeros((ch, ch), F32)
            row = (9 + i) * ch
            pack[row : row + ch, :] = jnp.concatenate([taps[2 * i][:, LANES:], second], axis=1)

    def unpack_taps(full, out):
        for i in range(9):
            tile = full[i * ch : (i + 1) * ch]
            out[3 * i] = tile[:, :ch]
            out[3 * i + 1] = tile[:, ch:]
            pair = full[(9 + i // 2) * ch : (10 + i // 2) * ch]
            out[3 * i + 2] = pair[:, :ch] if i % 2 == 0 else pair[:, ch:]

    class Reduce:
        def __init__(self, pack, wire, in_gz, part, mid, in_xy, full, sems):
            self.pack, self.wire, self.in_gz, self.part = pack, wire, in_gz, part
            self.mid, self.in_xy, self.full, self.sems = mid, in_xy, full, sems
            self.rows = pack.shape[0] // n_gz
            self.sub = self.rows // n_xy

        def copies(self, phase):
            result = []
            for k in range(1, n_gz if phase in (0, 3) else n_xy):
                if phase in (0, 3):
                    to = lax.rem(gz + k, n_gz)
                    target = (to, xy)
                else:
                    to = lax.rem(xy + k, n_xy)
                    target = (gz, to)
                source, landed = [
                    lambda: (self.wire.at[to], self.in_gz.at[k - 1]),
                    lambda: (self.mid.at[to], self.in_xy.at[k - 1]),
                    lambda: (self.full.at[gz, xy], self.full.at[gz, xy]),
                    lambda: (self.full.at[gz], self.full.at[gz]),
                ][phase]()
                result.append(
                    pltpu.make_async_remote_copy(
                        src_ref=source,
                        dst_ref=landed,
                        send_sem=self.sems.at[0, phase, k - 1],
                        recv_sem=self.sems.at[1, phase, k - 1],
                        device_id=target,
                        device_id_type=MESH,
                    )
                )
            return result

        def start(self, phase):
            for copy in self.copies(phase):
                copy.start()

        def finish(self, phase):
            for copy in self.copies(phase):
                copy.wait()

        def begin(self):
            for g in range(n_gz):
                self.wire[g] = self.pack[g * self.rows : (g + 1) * self.rows].astype(BF16)
            self.start(0)

        def second(self):
            self.finish(0)
            total = self.pack[pl.ds(pl.multiple_of(gz * self.rows, 16), self.rows), :]
            for k in range(n_gz - 1):
                total = total + self.in_gz[k].astype(F32)
            for j in range(n_xy):
                piece = total[j * self.sub : (j + 1) * self.sub]
                self.part[j] = piece
                self.mid[j] = piece.astype(BF16)
            self.start(1)

        def third(self):
            self.finish(1)
            total = self.part[xy]
            for k in range(n_xy - 1):
                total = total + self.in_xy[k].astype(F32)
            self.full[gz, xy] = total.astype(BF16)
            self.start(2)

        def fourth(self):
            self.finish(2)
            self.start(3)

        def done(self):
            self.finish(3)
            return self.full[...].astype(F32).reshape(self.rows * n_gz, LANES)

    sum_a = Reduce(pack_a, wire_a, in_a, part_a, mid_a, inx_a, full_a, sem_ra)
    sum_b = Reduce(pack_b, wire_b, in_b, part_b, mid_b, inx_b, full_b, sem_rb)

    lifted = []
    for a in range(2):
        pieces = []
        for y in range(ny):
            j, b = y // 2, y % 2
            row = (2 * a + b) * ch
            pieces.append(up[row : row + ch, j * LANES : (j + 1) * LANES])
        lifted.append((jnp.concatenate(pieces, axis=1) * plane_mask(a)).astype(BF16))
    send_halo(0, lifted)
    spread(0, lifted, s_lift)
    first = conv(a1, s_lift)
    acts = []
    for x in range(2):
        pre1[x] = first[x]
        acts.append((plane_mask(x) * first[x] * jax.nn.sigmoid(first[x])).astype(BF16))
    send_halo(1, acts)
    spread(1, acts, s_act)
    second = conv(a2, s_act)
    deltas = []
    for x in range(2):
        v = second[x]
        sig = jax.nn.sigmoid(v)
        m = plane_mask(x)
        dec[:, x * width : (x + 1) * width] = (m * (v * sig)).astype(BF16)
        slope = sig * (1.0 + v * (1.0 - sig))
        deltas.append((cot[:, x * width : (x + 1) * width].astype(F32) * m * slope).astype(BF16))

    send_halo(2, deltas)
    taps_two = tap_sums(deltas, s_act)
    pack_taps(taps_two, pack_a)
    used = 14 * ch
    pack_a[used:, :] = jnp.zeros((pack_a.shape[0] - used, LANES), F32)
    sum_a.begin()
    spread(2, deltas, s_grad)
    back = conv(b2, s_grad)
    deltas = []
    for x in range(2):
        v = pre1[x]
        sig = jax.nn.sigmoid(v)
        slope = sig * (1.0 + v * (1.0 - sig))
        deltas.append((back[x] * plane_mask(x) * slope).astype(BF16))
    send_halo(3, deltas)
    pack_taps(tap_sums(deltas, s_lift), pack_b)
    sum_a.second()
    spread(3, deltas, s_grad)
    back = conv(b1, s_grad)
    du = [(back[x] * plane_mask(x)).astype(BF16) for x in range(2)]
    stacked = jnp.concatenate(
        [
            jnp.concatenate([block(du[a], 2 * j + b) for j in range(ny // 2)], axis=1)
            for a in range(2)
            for b in range(2)
        ],
        axis=0,
    )
    pack_b[used : used + 4 * ch, :] = dot_nt(stacked, parents)
    rest = used + 4 * ch
    if pack_b.shape[0] > rest:
        pack_b[rest:, :] = jnp.zeros((pack_b.shape[0] - rest, LANES), F32)
    sum_b.begin()
    by_parity = dot_tn(wup[...], stacked)
    kept = jnp.where(even, by_parity[:ch], by_parity[ch:])
    paired = kept + pltpu.roll(kept, half - 1, 1)
    parent_grad = jnp.where(even, paired, jnp.zeros_like(paired)).astype(BF16)
    wide_grad = jnp.concatenate([parent_grad, jnp.zeros_like(parent_grad)], axis=0)
    slot_grad[...] = dot_nt(hot, wide_grad).astype(BF16).reshape(slot_grad.shape)
    each_device(lambda k: back_copy(k).start())
    ret[me] = slot_grad[0]
    sum_a.third()
    sum_b.second()
    sum_a.fourth()
    sum_b.third()
    each_device(lambda k: back_copy(k).wait())
    ret_out[...] = ret[...].reshape(slots, LANES).astype(F32).T[:ch].astype(BF16)
    unpack_taps(sum_a.done(), g2_out)
    sum_b.fourth()
    last = sum_b.done()
    unpack_taps(last, g1_out)
    for p in range(4):
        tile = last[used + p * ch : used + (p + 1) * ch]
        gup_out[2 * p] = tile[:, :ch]
        gup_out[2 * p + 1] = tile[:, ch:]
    for e in range(4):
        for side in range(8):
            there, copy = halo_copy(e, side)
            pl.when(there)(copy.wait_send)


def local(
    parent_feat, parent_cell, send_count, up_weight, conv_one, conv_two, child_mask, cotangent
):
    ch, size_x, ny, size_z = cotangent.shape
    n_gz, n_xy = lax.axis_size("gz"), lax.axis_size("xy")
    n_dev = n_gz * n_xy
    slot_total = parent_feat.shape[2]
    cap = slot_total // n_dev
    voxels = size_x * ny * size_z
    width = ny * size_z
    live = (jnp.arange(cap, dtype=jnp.int32)[None, :] < send_count[0][:, None]).reshape(slot_total)
    feats = jnp.where(live[None, :], parent_feat[0], jnp.zeros_like(parent_feat[0]))
    src = jnp.concatenate(
        [feats, parent_cell.astype(BF16), jnp.zeros((LANES - ch - 1, slot_total), BF16)], axis=0
    ).T.reshape(n_dev, cap, LANES)
    wup = up_weight.reshape(4, 2, ch, ch).transpose(0, 2, 1, 3).reshape(4 * ch, 2 * ch)
    mask = child_mask.astype(F32).reshape(1, voxels)
    cot = cotangent.reshape(ch, voxels)
    unit = n_dev * 16
    rows_a = -(-14 * ch // unit) * unit
    rows_b = -(-18 * ch // unit) * unit

    def reduce_scratch(rows):
        per = rows // n_gz
        sub = per // n_xy
        return [
            pltpu.VMEM((rows, LANES), F32),
            pltpu.VMEM((n_gz, per, LANES), BF16),
            pltpu.VMEM((n_gz - 1, per, LANES), BF16),
            pltpu.VMEM((n_xy, sub, LANES), F32),
            pltpu.VMEM((n_xy, sub, LANES), BF16),
            pltpu.VMEM((n_xy - 1, sub, LANES), BF16),
            pltpu.VMEM((n_gz, n_xy, sub, LANES), BF16),
        ]

    vmem = pl.BlockSpec(memory_space=pltpu.VMEM)
    most = max(n_gz, n_xy) - 1
    dma = pltpu.SemaphoreType.DMA
    dec, ret, g1, g2, gup = pl.pallas_call(
        functools.partial(all_kernel, (n_gz, n_xy, ch, ny)),
        out_shape=(
            jax.ShapeDtypeStruct((ch, voxels), BF16),
            jax.ShapeDtypeStruct((ch, slot_total), BF16),
            jax.ShapeDtypeStruct((27, ch, ch), F32),
            jax.ShapeDtypeStruct((27, ch, ch), F32),
            jax.ShapeDtypeStruct((8, ch, ch), F32),
        ),
        in_specs=[vmem] * 6,
        out_specs=(vmem,) * 5,
        scratch_shapes=[
            pltpu.VMEM((n_dev, cap, LANES), BF16),
            pltpu.VMEM((n_dev, cap, LANES), BF16),
            pltpu.VMEM((n_dev, cap, LANES), BF16),
            pltpu.VMEM((9 * ch, 3 * ch), BF16),
            pltpu.VMEM((9 * ch, 3 * ch), BF16),
            pltpu.VMEM((9 * ch, 3 * ch), BF16),
            pltpu.VMEM((9 * ch, 3 * ch), BF16),
            pltpu.VMEM((4, 2, ch, width), BF16),
            pltpu.VMEM((4, 2, ch, width), BF16),
            pltpu.VMEM((4, 2, ch, LANES), BF16),
            pltpu.VMEM((4, 6, ch, LANES), BF16),
            pltpu.VMEM((4, 3 * ch, width), BF16),
            pltpu.VMEM((4, 3 * ch, width), BF16),
            pltpu.VMEM((4, 3 * ch, width), BF16),
            pltpu.VMEM((2, ch, width + 2 * LANES), F32),
            pltpu.VMEM((2, ch, width + 2 * LANES), BF16),
            pltpu.VMEM((2, ch, width), F32),
            *reduce_scratch(rows_a),
            *reduce_scratch(rows_b),
            dma((2, n_dev)),
            dma((2, n_dev)),
            dma((2, 4, 8)),
            dma((2, 4, most)),
            dma((2, 4, most)),
        ],
        compiler_params=pltpu.CompilerParams(
            collective_id=0, has_side_effects=True, vmem_limit_bytes=56 * 1024 * 1024
        ),
    )(src, wup, conv_one, conv_two, mask, cot)
    decoded = dec.reshape(cotangent.shape)
    grad_parent = jnp.where(live[None, :], ret, jnp.zeros_like(ret))[None]
    scale = 1.0 / math.sqrt(size_x * n_xy * ny * size_z * n_gz)
    return (decoded, grad_parent, g1 * scale, g2 * scale, gup * scale)


def solution(mesh):
    placed = (
        P(("gz", "xy"), None, None),
        P(("gz", "xy"), None),
        P(("gz", "xy"), None),
        P(),
        P(),
        P(),
        P("xy", None, "gz"),
        P(None, "xy", None, "gz"),
    )
    return jax.shard_map(
        local,
        mesh=mesh,
        in_specs=placed,
        out_specs=(P(None, "xy", None, "gz"), P(("gz", "xy"), None, None), P(), P(), P()),
        check_vma=False,
    )
```

time: 387 us -> 88.5 us (0.23); the launches traced: 380 us -> 87.4 us
  waiting for transfers between devices: 165 us -> 0 us
  Pallas kernels: 0 us -> 74.3 us
  starting transfers between devices: 68.8 us -> 0 us
  matrix products: 64.9 us -> 0 us
  local copies, waits for them, and re-layouts: 40.9 us -> 5.08 us
  between operations: 16.9 us -> 0.71 us
  other arithmetic: 23 us -> 7.36 us
    psum x1 -> x0, waiting for transfers between devices: 120 us -> none  [local(): lax.psum((term_one, term_two, term_up), ('gz', 'xy'))]
    pallas_call x0 -> x1, Pallas kernels: none -> 74.3 us  [local(): pl.pallas_call(functools.partial(all_kernel, (n_gz, n_xy, ch, ny)), out_s...]
    dot_general x166 -> x0, matrix products: 64.9 us -> none  [the longest x108 49.9 us: convolve(): jnp.dot(orient(weights[index], direction), window(padded, offset, directi...]
    ppermute x16 -> x0, starting transfers between devices: 49.7 us -> none  [the longest x8 38.9 us: with_halo(): before = lax.ppermute(last, axis, up)]
    ppermute x16 -> x0, waiting for transfers between devices: 28.4 us -> none  [the longest x8 24.1 us: with_halo(): after = lax.ppermute(first, axis, down)]
    slice x116 -> x0, local copies, waits for them, and re-layouts: 25.1 us -> none  [the longest x108 23.1 us: window(): part = padded[:, 1 + ox:1 + ox + nx, 1 + oy:1 + oy + ny, 1 + oz:1 + oz + nz]]
    all_to_all x3 -> x0, starting transfers between devices: 19.1 us -> none  [the longest x1 9.23 us: local(): lax.all_to_all(slot_grad, ('gz', 'xy'), split_axis=1, concat_axis=1, tile...]
    all_to_all x3 -> x0, waiting for transfers between devices: 16.7 us -> none  [the longest x1 6.56 us: local(): lax.all_to_all(slot_grad, ('gz', 'xy'), split_axis=1, concat_axis=1, tile...]
  transfers between devices with their start and end apart: 20 -> 0, of which waited for: 16 -> 0; matrix products, arithmetic and copies ran while one was open for 3% -> 0% of each run, Pallas kernels for 0% -> 0%
where the time goes in v1:
time: 88.5 us; the launch traced here: 87.4 us
  Pallas kernels  74.3 us (84%)
  other arithmetic  7.36 us (8%)
  local copies, waits for them, and re-layouts  5.08 us (6%)
    pallas_call x1, Pallas kernels, local(): pl.pallas_call(functools.partial(all_kernel, (n_gz, n_xy, ch, ny)), out_s...  74.3 us
    mul x2, other arithmetic, local(): return (decoded, grad_parent, g1 * scale, g2 * scale, gup * scale)  4.26 us
    unnamed x14, local copies, waits for them, and re-layouts  3.26 us

profile of v1, /device:TPU:0, one launch (start us, length us, event | category | flops | bytes accessed | tf_op | source)
XLA Modules:
  0.0 87.4 jit_solution(6728843921656946104)
XLA Ops:
  0.6 0.0 copy-start.4
  0.6 0.0 copy-start.5
  0.7 0.0 copy-start.3
  0.7 0.1 pad.2.clone
  0.7 0.6 copy-done.4
  1.3 0.0 copy-done.5
  1.3 0.1 iota_compare_fusion
  1.4 0.1 lt.26
  1.5 0.0 copy-done.3
  1.5 0.6 convert_element_type.7
  2.1 0.8 bitcast_select_fusion
  2.9 0.1 maximum_bitcast_fusion
  3.0 0.0 copy-start.2
  3.1 0.8 copy.15
  3.8 0.0 copy-start.1
  3.8 0.1 copy-done.2
  3.9 0.1 copy.22
  4.1 0.7 reshape.45.wup
  4.8 0.0 copy-done.1
  4.8 0.8 copy.21
  5.6 74.3 %shard_map.119 = (bf16[64,2048]{1,0:T(8,128)(2,1)}, bf16[64,512]{1,0:T(8,128)(2,1)}, f32[27,64,64]{2,1,0:T(8,128)}, f32[27,64,64]{2,1,0:T(8,128)}, f32[8,64,64]{2,1,0:T(8,128)}) custom-call(bf16[32,16,128]{2,1,0:T(8,128)(2,1)} %bitcast.23, bf16[256,128]{1,0:T(8,128)(2,1)} %reshape.45.wup, bf16[27,64,64]{2,1,0:T(8,128)(2,1)} %w1.1, bf16[27,64,64]{2,1,0:T(8,128)(2,1)} %w2.1, ...), custom_call_target="tpu_custom_call" | custom-call | tf_op jit(solution)/shard_map/pallas_call | solution.py:465
  79.9 0.0 copy-start
  79.9 1.8 %copy.18 = bf16[8,8,16,128]{3,2,1,0:T(8,128)(2,1)} copy(bf16[8,8,16,128]{3,1,2,0:T(8,128)(2,1)} %bitcast.26) | data formatting | bytes 524288
  81.7 1.5 %select_bitcast_fusion = bf16[1,64,512]{2,1,0:T(8,128)(2,1)} fusion(bf16[64,512]{1,0:T(8,128)(2,1)} %get-tuple-element.11, pred[512]{0:T(512)(128)(4,1)S(1)} %lt.26), kind=kLoop, calls=%fused_computation.7 | loop fusion | flops 32768 | bytes 131584 | tf_op jit(solution)/shard_map/broadcast_in_dim | solution.py:507
  83.2 1.7 %broadcast_multiply_fusion.2 = f32[8,64,64]{2,1,0:T(8,128)} fusion(f32[8,64,64]{2,1,0:T(8,128)} %get-tuple-element.14), kind=kLoop, calls=%fused_computation.5 | loop fusion | flops 32768 | bytes 262144 | tf_op jit(solution)/shard_map/mul | solution.py:509
  84.8 0.0 copy-done
  84.8 2.6 %broadcast_multiply_fusion = (f32[27,64,64]{2,1,0:T(8,128)}, f32[27,64,64]{2,1,0:T(8,128)}) fusion(f32[27,64,64]{2,1,0:T(8,128)} %get-tuple-element.13, f32[27,64,64]{2,1,0:T(8,128)S(1)} %copy-done), kind=kLoop, calls=%fused_computation | loop fusion | flops 221184 | bytes 1769472 | tf_op jit(solution)/shard_map/mul | solution.py:509
  (2 shorter events, 0.0 us)
Async XLA Ops:
  0.6 0.7 copy-start.4
  0.6 0.7 copy-start.5
  0.7 0.8 copy-start.3
  3.0 0.9 %copy-start.2 = (bf16[8,64,64]{2,1,0:T(8,128)(2,1)S(1)}, bf16[8,64,64]{2,1,0:T(8,128)(2,1)}, u32[]{:S(2)}) copy-start(bf16[8,64,64]{2,1,0:T(8,128)(2,1)} %param.11) | copy-start | bytes 196612
  3.8 1.0 %copy-start.1 = (bf16[64,2,8,128]{3,2,1,0:T(8,128)(2,1)S(1)}, bf16[64,2,8,128]{3,2,1,0:T(8,128)(2,1)}, u32[]{:S(2)}) copy-start(bf16[64,2,8,128]{3,2,1,0:T(8,128)(2,1)} %param.15) | copy-start | bytes 786436
  79.9 4.9 %copy-start = (f32[27,64,64]{2,1,0:T(8,128)S(1)}, f32[27,64,64]{2,1,0:T(8,128)}, u32[]{:S(2)}) copy-start(f32[27,64,64]{2,1,0:T(8,128)} %get-tuple-element.12) | copy-start | bytes 1327108

commit v2 on v1

--- a/solution.py
+++ b/solution.py
@@ -29,9 +29,9 @@
 
 def all_kernel(
     dims,
-    src, wup, w1, w2, mask, cot,
-    dec, ret_out, g1_out, g2_out, gup_out,
-    got, slot_grad, ret,
+    feat, cell, count, w_up, w1, w2, mask_in, cot_in,
+    dec, ret_out, out_a, out_b,
+    src, wup, got, slot_grad, ret,
     a1, b1, a2, b2,
     planes, plane_in, tile_out, tile_in,
     s_lift, s_act, s_grad, acc, dpad, pre1,
@@ -101,6 +101,24 @@
                 ref[...] = jnp.zeros(ref.shape, BF16)
 
     dpad[...] = jnp.zeros(dpad.shape, BF16)
+    slots = got.shape[0] * got.shape[1]
+    cap = got.shape[1]
+    slot = lax.broadcasted_iota(jnp.int32, (1, slots), 1)
+    to_slot = lax.broadcasted_iota(jnp.int32, (n_dev, slots), 0) == slot // cap
+    counts = jnp.broadcast_to(count[...].astype(F32), (8, n_dev)).astype(BF16)
+    counts = dot(counts, jnp.where(to_slot, 1.0, 0.0).astype(BF16))[:1]
+    live = lax.rem(slot, cap).astype(F32) < counts
+    sent = jnp.concatenate(
+        [
+            jnp.where(live, feat[0].astype(F32), 0.0),
+            jnp.broadcast_to(cell[...].astype(F32), (8, slots)),
+            jnp.zeros((LANES - ch - 8, slots), F32),
+        ],
+        axis=0,
+    )
+    src[...] = sent.T.astype(BF16).reshape(src.shape)
+    for i in range(4):
+        wup[i * ch : (i + 1) * ch, :] = jnp.concatenate([w_up[2 * i], w_up[2 * i + 1]], axis=1)
     pl.semaphore_wait(barrier, n_dev - 1)
 
     def to_copy(k):
@@ -137,7 +155,6 @@
     lax.fori_loop(0, 9, weights, 0)
     each_device(lambda k: to_copy(k).wait())
 
-    slots = got.shape[0] * got.shape[1]
     listed = got[...].reshape(slots, LANES)
     half = 4 * LANES
     column = lax.broadcasted_iota(jnp.int32, (1, half), 1)
@@ -158,7 +175,11 @@
         return value[:, y * LANES : (y + 1) * LANES]
 
     def plane_mask(x):
-        return mask[:, x * width : (x + 1) * width]
+        rows = mask_in[x].astype(F32)
+        return jnp.concatenate([rows[y : y + 1] for y in range(ny)], axis=1)
+
+    def cot_plane(x):
+        return cot_in[:, x].astype(F32).reshape(ch, width)
 
     def send_halo(e, fields):
         edge = lax.rem(lane, 16)
@@ -182,24 +203,22 @@
             there, copy = halo_copy(e, side)
             pl.when(there)(copy.start)
 
-    def spread(e, fields, into):
-        for side, (dx, dz) in enumerate(SIDES):
-            has_source, _ = near(-dx, -dz)
-            _, copy = halo_copy(e, side)
-            pl.when(has_source)(copy.wait_recv)
-
-        def edges(base):
-            after, same, before = [tile_in[e, base + t].astype(F32) for t in range(3)]
-            return jnp.where(lane < 8, before, jnp.where(lane < 24, same, after))
-
-        low, high = edges(0), edges(3)
-        for xp in range(4):
-            if xp in (1, 2):
-                field = fields[xp - 1]
-            else:
-                field = plane_in[e, 0 if xp == 0 else 1]
+    REACH = [(-1,), (-1, 0), (0, 1), (1,)]
+
+    def conv(e, fields, held, matrix):
+        def arrive(sides):
+            for side in sides:
+                dx, dz = SIDES[side]
+                has_source, _ = near(-dx, -dz)
+                _, copy = halo_copy(e, side)
+                pl.when(has_source)(copy.wait_recv)
+
+        def tile(side):
+            return tile_in[e, side - 2].astype(F32)
+
+        def spread(xp, field, low, high):
             wide = field.astype(F32)
-            into[xp, ch : 2 * ch, :] = field
+            held[xp, ch : 2 * ch, :] = field
             for y in range(ny):
                 part = block(wide, y)
                 at = xp * 8 + y
@@ -208,14 +227,10 @@
                     lane == LANES - 1, high[:, at : at + 1], pltpu.roll(part, LANES - 1, 1)
                 )
                 cols = slice(y * LANES, (y + 1) * LANES)
-                into[xp, 0:ch, cols] = left.astype(BF16)
-                into[xp, 2 * ch : 3 * ch, cols] = right.astype(BF16)
-
-    REACH = [(-1,), (-1, 0), (0, 1), (1,)]
-
-    def conv(matrix, held):
-        acc[...] = jnp.zeros(acc.shape, F32)
-        for xp in range(4):
+                held[xp, 0:ch, cols] = left.astype(BF16)
+                held[xp, 2 * ch : 3 * ch, cols] = right.astype(BF16)
+
+        def add(xp):
             steps = REACH[xp]
             low = 3 * ch * (steps[0] + 1)
             product = dot(matrix[low : low + 3 * ch * len(steps), :], held[xp])
@@ -225,6 +240,18 @@
                     row = (3 * n + oy + 1) * ch
                     cols = slice((1 - oy) * LANES, (1 - oy) * LANES + width)
                     acc[x, :, cols] += product[row : row + ch]
+
+        acc[...] = jnp.zeros(acc.shape, F32)
+        arrive((3, 6))
+        low, high = tile(3), tile(6)
+        for xp in (1, 2):
+            spread(xp, fields[xp - 1], low, high)
+            add(xp)
+        arrive((0, 1, 2, 4, 5, 7))
+        spread(0, plane_in[e, 0], tile(4), tile(7))
+        add(0)
+        spread(3, plane_in[e, 1], tile(2), tile(5))
+        add(3)
         return [acc[x, :, LANES : LANES + width] for x in range(2)]
 
     def tap_sums(deltas, held):
@@ -250,14 +277,6 @@
             second = taps[2 * i + 1][:, LANES:] if i < 4 else jnp.zeros((ch, ch), F32)
             row = (9 + i) * ch
             pack[row : row + ch, :] = jnp.concatenate([taps[2 * i][:, LANES:], second], axis=1)
-
-    def unpack_taps(full, out):
-        for i in range(9):
-            tile = full[i * ch : (i + 1) * ch]
-            out[3 * i] = tile[:, :ch]
-            out[3 * i + 1] = tile[:, ch:]
-            pair = full[(9 + i // 2) * ch : (10 + i // 2) * ch]
-            out[3 * i + 2] = pair[:, :ch] if i % 2 == 0 else pair[:, ch:]
 
     class Reduce:
         def __init__(self, pack, wire, in_gz, part, mid, in_xy, full, sems):
@@ -331,7 +350,7 @@
 
         def done(self):
             self.finish(3)
-            return self.full[...].astype(F32).reshape(self.rows * n_gz, LANES)
+            return self.full[...].reshape(self.rows * n_gz, LANES)
 
     sum_a = Reduce(pack_a, wire_a, in_a, part_a, mid_a, inx_a, full_a, sem_ra)
     sum_b = Reduce(pack_b, wire_b, in_b, part_b, mid_b, inx_b, full_b, sem_rb)
@@ -345,15 +364,13 @@
             pieces.append(up[row : row + ch, j * LANES : (j + 1) * LANES])
         lifted.append((jnp.concatenate(pieces, axis=1) * plane_mask(a)).astype(BF16))
     send_halo(0, lifted)
-    spread(0, lifted, s_lift)
-    first = conv(a1, s_lift)
+    first = conv(0, lifted, s_lift, a1)
     acts = []
     for x in range(2):
         pre1[x] = first[x]
         acts.append((plane_mask(x) * first[x] * jax.nn.sigmoid(first[x])).astype(BF16))
     send_halo(1, acts)
-    spread(1, acts, s_act)
-    second = conv(a2, s_act)
+    second = conv(1, acts, s_act, a2)
     deltas = []
     for x in range(2):
         v = second[x]
@@ -361,7 +378,7 @@
         m = plane_mask(x)
         dec[:, x * width : (x + 1) * width] = (m * (v * sig)).astype(BF16)
         slope = sig * (1.0 + v * (1.0 - sig))
-        deltas.append((cot[:, x * width : (x + 1) * width].astype(F32) * m * slope).astype(BF16))
+        deltas.append((cot_plane(x) * m * slope).astype(BF16))
 
     send_halo(2, deltas)
     taps_two = tap_sums(deltas, s_act)
@@ -369,8 +386,7 @@
     used = 14 * ch
     pack_a[used:, :] = jnp.zeros((pack_a.shape[0] - used, LANES), F32)
     sum_a.begin()
-    spread(2, deltas, s_grad)
-    back = conv(b2, s_grad)
+    back = conv(2, deltas, s_grad, b2)
     deltas = []
     for x in range(2):
         v = pre1[x]
@@ -380,8 +396,7 @@
     send_halo(3, deltas)
     pack_taps(tap_sums(deltas, s_lift), pack_b)
     sum_a.second()
-    spread(3, deltas, s_grad)
-    back = conv(b1, s_grad)
+    back = conv(3, deltas, s_grad, b1)
     du = [(back[x] * plane_mask(x)).astype(BF16) for x in range(2)]
     stacked = jnp.concatenate(
         [
@@ -409,19 +424,35 @@
     sum_a.fourth()
     sum_b.third()
     each_device(lambda k: back_copy(k).wait())
-    ret_out[...] = ret[...].reshape(slots, LANES).astype(F32).T[:ch].astype(BF16)
-    unpack_taps(sum_a.done(), g2_out)
+    returned = ret[...].reshape(slots, LANES).astype(F32).T[:ch]
+    ret_out[...] = jnp.where(live, returned, 0.0).astype(BF16)
+    out_a[...] = sum_a.done()
     sum_b.fourth()
-    last = sum_b.done()
-    unpack_taps(last, g1_out)
-    for p in range(4):
-        tile = last[used + p * ch : used + (p + 1) * ch]
-        gup_out[2 * p] = tile[:, :ch]
-        gup_out[2 * p + 1] = tile[:, ch:]
+    out_b[...] = sum_b.done()
     for e in range(4):
         for side in range(8):
             there, copy = halo_copy(e, side)
             pl.when(there)(copy.wait_send)
+
+
+def finish_kernel(scale, dims, dec, ret, full_a, full_b, dec_out, ret_out, g1_out, g2_out, gup_out):
+    ch, ny = dims
+    width = ny * LANES
+    for x in range(2):
+        plane = dec[:, x * width : (x + 1) * width].astype(F32)
+        dec_out[:, x] = plane.reshape(ch, ny, LANES).astype(BF16)
+    ret_out[0] = ret[...]
+    for full, out in ((full_b, g1_out), (full_a, g2_out)):
+        for i in range(9):
+            tile = full[i * ch : (i + 1) * ch].astype(F32) * scale
+            out[3 * i] = tile[:, :ch]
+            out[3 * i + 1] = tile[:, ch:]
+            pair = full[(9 + i // 2) * ch : (10 + i // 2) * ch].astype(F32) * scale
+            out[3 * i + 2] = pair[:, :ch] if i % 2 == 0 else pair[:, ch:]
+    for p in range(4):
+        tile = full_b[(14 + p) * ch : (15 + p) * ch].astype(F32) * scale
+        gup_out[2 * p] = tile[:, :ch]
+        gup_out[2 * p + 1] = tile[:, ch:]
 
 
 def local(
@@ -434,14 +465,6 @@
     cap = slot_total // n_dev
     voxels = size_x * ny * size_z
     width = ny * size_z
-    live = (jnp.arange(cap, dtype=jnp.int32)[None, :] < send_count[0][:, None]).reshape(slot_total)
-    feats = jnp.where(live[None, :], parent_feat[0], jnp.zeros_like(parent_feat[0]))
-    src = jnp.concatenate(
-        [feats, parent_cell.astype(BF16), jnp.zeros((LANES - ch - 1, slot_total), BF16)], axis=0
-    ).T.reshape(n_dev, cap, LANES)
-    wup = up_weight.reshape(4, 2, ch, ch).transpose(0, 2, 1, 3).reshape(4 * ch, 2 * ch)
-    mask = child_mask.astype(F32).reshape(1, voxels)
-    cot = cotangent.reshape(ch, voxels)
     unit = n_dev * 16
     rows_a = -(-14 * ch // unit) * unit
     rows_b = -(-18 * ch // unit) * unit
@@ -462,18 +485,19 @@
     vmem = pl.BlockSpec(memory_space=pltpu.VMEM)
     most = max(n_gz, n_xy) - 1
     dma = pltpu.SemaphoreType.DMA
-    dec, ret, g1, g2, gup = pl.pallas_call(
+    dec, ret, full_a, full_b = pl.pallas_call(
         functools.partial(all_kernel, (n_gz, n_xy, ch, ny)),
         out_shape=(
             jax.ShapeDtypeStruct((ch, voxels), BF16),
             jax.ShapeDtypeStruct((ch, slot_total), BF16),
-            jax.ShapeDtypeStruct((27, ch, ch), F32),
-            jax.ShapeDtypeStruct((27, ch, ch), F32),
-            jax.ShapeDtypeStruct((8, ch, ch), F32),
+            jax.ShapeDtypeStruct((rows_a, LANES), BF16),
+            jax.ShapeDtypeStruct((rows_b, LANES), BF16),
         ),
-        in_specs=[vmem] * 6,
-        out_specs=(vmem,) * 5,
+        in_specs=[vmem] * 8,
+        out_specs=(vmem,) * 4,
         scratch_shapes=[
+            pltpu.VMEM((n_dev, cap, LANES), BF16),
+            pltpu.VMEM((4 * ch, 2 * ch), BF16),
             pltpu.VMEM((n_dev, cap, LANES), BF16),
             pltpu.VMEM((n_dev, cap, LANES), BF16),
             pltpu.VMEM((n_dev, cap, LANES), BF16),
@@ -502,11 +526,20 @@
         compiler_params=pltpu.CompilerParams(
             collective_id=0, has_side_effects=True, vmem_limit_bytes=56 * 1024 * 1024
         ),
-    )(src, wup, conv_one, conv_two, mask, cot)
-    decoded = dec.reshape(cotangent.shape)
-    grad_parent = jnp.where(live[None, :], ret, jnp.zeros_like(ret))[None]
+    )(parent_feat, parent_cell, send_count, up_weight, conv_one, conv_two, child_mask, cotangent)
     scale = 1.0 / math.sqrt(size_x * n_xy * ny * size_z * n_gz)
-    return (decoded, grad_parent, g1 * scale, g2 * scale, gup * scale)
+    return pl.pallas_call(
+        functools.partial(finish_kernel, scale, (ch, ny)),
+        out_shape=(
+            jax.ShapeDtypeStruct(cotangent.shape, BF16),
+            jax.ShapeDtypeStruct((1, ch, slot_total), BF16),
+            jax.ShapeDtypeStruct((27, ch, ch), F32),
+            jax.ShapeDtypeStruct((27, ch, ch), F32),
+            jax.ShapeDtypeStruct((8, ch, ch), F32),
+        ),
+        in_specs=[vmem] * 4,
+        out_specs=(vmem,) * 5,
+    )(dec, ret, full_a, full_b)
 
 
 def solution(mesh):

time: 88.5 us -> 75.6 us (0.85)
  other arithmetic: 7.36 us -> 0 us
  local copies, waits for them, and re-layouts: 5.08 us -> 0 us
    mul x2 -> x0, other arithmetic: 4.26 us -> none  [local(): return (decoded, grad_parent, g1 * scale, g2 * scale, gup * scale)]
    unnamed x14 -> x0, local copies, waits for them, and re-layouts: 3.26 us -> none
    pallas_call x0 -> x1, Pallas kernels: none -> 2.86 us  [local(): pl.pallas_call(functools.partial(finish_kernel, scale, (ch, ny)), out_sha...]
    pallas_call x1, Pallas kernels: 74.3 us -> 71.6 us  [local(): pl.pallas_call(functools.partial(all_kernel, (n_gz, n_xy, ch, ny)), out_s...]
    broadcast_in_dim x1 -> x0, other arithmetic: 1.48 us -> none  [local(): grad_parent = jnp.where(live[None, :], ret, jnp.zeros_like(ret))[None]]
where the time goes in v2:
time: 75.6 us; the launch traced here: 75.1 us
  Pallas kernels  74.4 us (98%)
    pallas_call x1, Pallas kernels, local(): pl.pallas_call(functools.partial(all_kernel, (n_gz, n_xy, ch, ny)), out_s...  71.6 us
    pallas_call x1, Pallas kernels, local(): pl.pallas_call(functools.partial(finish_kernel, scale, (ch, ny)), out_sha...  2.86 us

profile of v2, /device:TPU:0, one launch (start us, length us, event | category | flops | bytes accessed | tf_op | source)
XLA Modules:
  0.0 75.1 jit_solution(1985997565233808379)
XLA Ops:
  0.6 71.6 %shard_map.119 = (bf16[64,2048]{1,0:T(8,128)(2,1)}, bf16[64,512]{1,0:T(8,128)(2,1)}, bf16[1024,128]{1,0:T(8,128)(2,1)}, bf16[1536,128]{1,0:T(8,128)(2,1)}) custom-call(bf16[1,64,512]{2,1,0:T(8,128)(2,1)} %feat.1, s32[1,512]{1,0:T(1,128)} %cell.1, s32[1,32]{1,0:T(1,128)} %count.1, bf16[8,64,64]{2,1,0:T(8,128)(2,1)} %w_up.1, bf16[27,64,64]{2,1,0:T(8,128)(2,1)} %w1.1, ...), custom_call_target="tpu_custom_call" | custom-call | tf_op jit(solution)/shard_map/pallas_call | solution.py:488
  72.2 2.9 %shard_map.120 = (bf16[64,2,8,128]{3,2,1,0:T(8,128)(2,1)}, bf16[1,64,512]{2,1,0:T(8,128)(2,1)}, f32[27,64,64]{2,1,0:T(8,128)}, f32[27,64,64]{2,1,0:T(8,128)}, f32[8,64,64]{2,1,0:T(8,128)}) custom-call(bf16[64,2048]{1,0:T(8,128)(2,1)} %get-tuple-element.9.dec, bf16[64,512]{1,0:T(8,128)(2,1)} %get-tuple-element.10.ret, ...), custom_call_target="tpu_custom_call" | custom-call | tf_op jit(solution)/shard_map/pallas_call | solution.py:531

commit v3 on v2

--- a/solution.py
+++ b/solution.py
@@ -12,6 +12,7 @@
 F32 = jnp.float32
 BF16 = jnp.bfloat16
 LANES = 128
+USED = [range(8), (3, 6), range(8), range(8), (0, 1)]
 SIDES = [(1, 0), (-1, 0), (-1, 1), (0, 1), (1, 1), (-1, -1), (0, -1), (1, -1)]
 
 
@@ -30,14 +31,16 @@
 def all_kernel(
     dims,
     feat, cell, count, w_up, w1, w2, mask_in, cot_in,
-    dec, ret_out, out_a, out_b,
+    dec, ret_out, out_a, out_b, out_c,
     src, wup, got, slot_grad, ret,
     a1, b1, a2, b2,
+    grid, grid_in, mask_out, mask_halo,
     planes, plane_in, tile_out, tile_in,
     s_lift, s_act, s_grad, acc, dpad, pre1,
     pack_a, wire_a, in_a, part_a, mid_a, inx_a, full_a,
     pack_b, wire_b, in_b, part_b, mid_b, inx_b, full_b,
-    sem_to, sem_back, sem_halo, sem_ra, sem_rb,
+    pack_c, in_c, full_c,
+    sem_to, sem_back, sem_halo, sem_ra, sem_rb, sem_c,
 ):
     n_gz, n_xy, ch, ny = dims
     n_dev = n_gz * n_xy
@@ -73,13 +76,19 @@
 
     def landing(e, side):
         dx, dz = SIDES[side]
-        return plane_in.at[e, side] if dz == 0 else tile_in.at[e, side - 2]
+        if dz != 0:
+            return tile_in.at[e, side - 2]
+        return {0: grid_in, 4: mask_halo}[e].at[side] if e in (0, 4) else plane_in.at[e - 2, side]
 
     def halo_copy(e, side):
         dx, dz = SIDES[side]
         there, target = near(dx, dz)
-        if dz == 0:
-            source = planes.at[e, 1 if dx > 0 else 0]
+        if e == 0 and dz == 0:
+            source = grid
+        elif e == 4:
+            source = mask_out
+        elif dz == 0:
+            source = planes.at[e - 2, 1 if dx > 0 else 0]
         else:
             source = tile_out.at[e, 1 if dz > 0 else 0]
         return there, pltpu.make_async_remote_copy(
@@ -96,7 +105,7 @@
 
         @pl.when(jnp.logical_not(has_source))
         def _():
-            for e in range(4):
+            for e in [e for e in range(5) if side in USED[e]]:
                 ref = landing(e, side)
                 ref[...] = jnp.zeros(ref.shape, BF16)
 
@@ -119,6 +128,7 @@
     src[...] = sent.T.astype(BF16).reshape(src.shape)
     for i in range(4):
         wup[i * ch : (i + 1) * ch, :] = jnp.concatenate([w_up[2 * i], w_up[2 * i + 1]], axis=1)
+    mask_out[...] = jnp.concatenate([mask_in[0], mask_in[1]], axis=0).astype(F32).astype(BF16)
     pl.semaphore_wait(barrier, n_dev - 1)
 
     def to_copy(k):
@@ -151,23 +161,54 @@
         lax.fori_loop(1, n_dev, step, 0)
 
     each_device(lambda k: to_copy(k).start())
+    for side in USED[4]:
+        there, copy = halo_copy(4, side)
+        pl.when(there)(copy.start)
     got[0] = src[me]
     lax.fori_loop(0, 9, weights, 0)
     each_device(lambda k: to_copy(k).wait())
 
     listed = got[...].reshape(slots, LANES)
     half = 4 * LANES
+    cells = listed[:, ch : ch + 1].astype(F32)
+    owner = lax.broadcasted_iota(jnp.int32, (1, half // 2), 1).astype(F32)
+    hot = jnp.where(cells == owner, 1.0, 0.0).astype(BF16)
+    grid[...] = dot_tn(listed, hot)[:ch].astype(BF16)
+    for side in (0, 1):
+        there, copy = halo_copy(0, side)
+        pl.when(there)(copy.start)
     column = lax.broadcasted_iota(jnp.int32, (1, half), 1)
-    owner = (column // LANES) * (LANES // 2) + lax.rem(column, LANES) // 2
-    cells = listed[:, ch : ch + 1].astype(F32)
-    hot = jnp.where(cells == owner.astype(F32), 1.0, 0.0).astype(BF16)
-    grid_twice = dot_tn(listed, hot)[:ch]
     even = lax.rem(column, 2) == 0
-    none = jnp.zeros_like(grid_twice)
-    parents = jnp.concatenate(
-        [jnp.where(even, grid_twice, none), jnp.where(even, none, grid_twice)], axis=0
+    twice = jnp.where(
+        lax.broadcasted_iota(jnp.int32, (LANES, 2 * LANES), 0)
+        == lax.broadcasted_iota(jnp.int32, (LANES, 2 * LANES), 1) // 2,
+        1.0,
+        0.0,
     ).astype(BF16)
-    up = dot(wup[...], parents)
+
+    def by_parity_of(values):
+        wide = jnp.concatenate([dot(values[:, :LANES], twice), dot(values[:, LANES:], twice)], axis=1)
+        none = jnp.zeros_like(wide)
+        return jnp.concatenate(
+            [jnp.where(even, wide, none), jnp.where(even, none, wide)], axis=0
+        ).astype(BF16)
+
+    def mask_row(tile, x):
+        return jnp.concatenate([tile[x * ny + y : x * ny + y + 1] for y in range(ny)], axis=1)
+
+    def lift(listed_parents, tile):
+        up = dot(wup[...], listed_parents)
+        result = []
+        for a in range(2):
+            pieces = []
+            for y in range(ny):
+                row = (2 * a + y % 2) * ch
+                pieces.append(up[row : row + ch, (y // 2) * LANES : (y // 2 + 1) * LANES])
+            result.append((jnp.concatenate(pieces, axis=1) * mask_row(tile, a)).astype(BF16))
+        return result
+
+    parents = by_parity_of(grid[...])
+    own_mask = mask_out[...].astype(F32)
 
     lane = lax.broadcasted_iota(jnp.int32, (1, LANES), 1)
 
@@ -175,97 +216,104 @@
         return value[:, y * LANES : (y + 1) * LANES]
 
     def plane_mask(x):
-        rows = mask_in[x].astype(F32)
-        return jnp.concatenate([rows[y : y + 1] for y in range(ny)], axis=1)
+        return mask_row(own_mask, x)
 
     def cot_plane(x):
         return cot_in[:, x].astype(F32).reshape(ch, width)
 
-    def send_halo(e, fields):
-        edge = lax.rem(lane, 16)
-        first = jnp.zeros((ch, LANES), F32)
-        last = jnp.zeros((ch, LANES), F32)
+    def send_planes(e, fields):
         for x in range(2):
-            planes[e, x] = fields[x]
+            planes[e - 2, x] = fields[x]
         for side in (0, 1):
             there, copy = halo_copy(e, side)
             pl.when(there)(copy.start)
-        for x in range(2):
-            wide = fields[x].astype(F32)
+
+    def send_edges(e, fields, shift):
+        period = len(fields) * ny
+        edge = lax.rem(lane, period)
+        first = jnp.zeros((ch, LANES), F32)
+        last = jnp.zeros((ch, LANES), F32)
+        for x, field in enumerate(fields):
+            wide = field.astype(F32)
             for y in range(ny):
-                here = edge == (8 + x * 8 + y) % 16
+                here = edge == (shift + x * ny + y) % period
                 part = block(wide, y)
                 first = jnp.where(here, part[:, :1], first)
                 last = jnp.where(here, part[:, LANES - 1 :], last)
         tile_out[e, 0] = first.astype(BF16)
         tile_out[e, 1] = last.astype(BF16)
-        for side in range(2, 8):
-            there, copy = halo_copy(e, side)
-            pl.when(there)(copy.start)
-
-    REACH = [(-1,), (-1, 0), (0, 1), (1,)]
+        for side in (3, 6, 2, 4, 5, 7):
+            if side in USED[e]:
+                there, copy = halo_copy(e, side)
+                pl.when(there)(copy.start)
+
+    def arrive(e, sides):
+        for side in sides:
+            dx, dz = SIDES[side]
+            has_source, _ = near(-dx, -dz)
+            _, copy = halo_copy(e, side)
+            pl.when(has_source)(copy.wait_recv)
+
+    def tile(e, side):
+        return tile_in[e, side - 2].astype(F32)
+
+    def spread(held, xp, field, low, high):
+        wide = field.astype(F32)
+        held[xp, ch : 2 * ch, :] = field
+        for y in range(ny):
+            part = block(wide, y)
+            at = xp * ny + y
+            left = jnp.where(lane == 0, low[:, at : at + 1], pltpu.roll(part, 1, 1))
+            right = jnp.where(
+                lane == LANES - 1, high[:, at : at + 1], pltpu.roll(part, LANES - 1, 1)
+            )
+            cols = slice(y * LANES, (y + 1) * LANES)
+            held[xp, 0:ch, cols] = left.astype(BF16)
+            held[xp, 2 * ch : 3 * ch, cols] = right.astype(BF16)
+
+    def reach(xp, count):
+        return [ox for ox in (-1, 0, 1) if 0 <= xp - 1 - ox < count]
+
+    def add(matrix, held, xp, count):
+        steps = reach(xp, count)
+        low = 3 * ch * (steps[0] + 1)
+        product = dot(matrix[low : low + 3 * ch * len(steps), :], held[xp])
+        for n, ox in enumerate(steps):
+            x = xp - 1 - ox
+            for oy in (-1, 0, 1):
+                row = (3 * n + oy + 1) * ch
+                cols = slice((1 - oy) * LANES, (1 - oy) * LANES + width)
+                acc[x, :, cols] += product[row : row + ch]
+
+    def result(count):
+        return [acc[x, :, LANES : LANES + width] for x in range(count)]
 
     def conv(e, fields, held, matrix):
-        def arrive(sides):
-            for side in sides:
-                dx, dz = SIDES[side]
-                has_source, _ = near(-dx, -dz)
-                _, copy = halo_copy(e, side)
-                pl.when(has_source)(copy.wait_recv)
-
-        def tile(side):
-            return tile_in[e, side - 2].astype(F32)
-
-        def spread(xp, field, low, high):
-            wide = field.astype(F32)
-            held[xp, ch : 2 * ch, :] = field
-            for y in range(ny):
-                part = block(wide, y)
-                at = xp * 8 + y
-                left = jnp.where(lane == 0, low[:, at : at + 1], pltpu.roll(part, 1, 1))
-                right = jnp.where(
-                    lane == LANES - 1, high[:, at : at + 1], pltpu.roll(part, LANES - 1, 1)
-                )
-                cols = slice(y * LANES, (y + 1) * LANES)
-                held[xp, 0:ch, cols] = left.astype(BF16)
-                held[xp, 2 * ch : 3 * ch, cols] = right.astype(BF16)
-
-        def add(xp):
-            steps = REACH[xp]
-            low = 3 * ch * (steps[0] + 1)
-            product = dot(matrix[low : low + 3 * ch * len(steps), :], held[xp])
-            for n, ox in enumerate(steps):
-                x = xp - 1 - ox
-                for oy in (-1, 0, 1):
-                    row = (3 * n + oy + 1) * ch
-                    cols = slice((1 - oy) * LANES, (1 - oy) * LANES + width)
-                    acc[x, :, cols] += product[row : row + ch]
-
         acc[...] = jnp.zeros(acc.shape, F32)
-        arrive((3, 6))
-        low, high = tile(3), tile(6)
+        arrive(e, (3, 6))
+        low, high = tile(e, 3), tile(e, 6)
         for xp in (1, 2):
-            spread(xp, fields[xp - 1], low, high)
-            add(xp)
-        arrive((0, 1, 2, 4, 5, 7))
-        spread(0, plane_in[e, 0], tile(4), tile(7))
-        add(0)
-        spread(3, plane_in[e, 1], tile(2), tile(5))
-        add(3)
-        return [acc[x, :, LANES : LANES + width] for x in range(2)]
-
-    def tap_sums(deltas, held):
+            spread(held, xp, fields[xp - 1], low, high)
+            add(matrix, held, xp, 2)
+        arrive(e, (0, 1, 2, 4, 5, 7))
+        spread(held, 0, plane_in[e - 2, 0], tile(e, 4), tile(e, 7))
+        add(matrix, held, 0, 2)
+        spread(held, 3, plane_in[e - 2, 1], tile(e, 2), tile(e, 5))
+        add(matrix, held, 3, 2)
+        return result(2)
+
+    def tap_sums(deltas, held, start):
         for x in range(2):
             dpad[x, :, LANES : LANES + width] = deltas[x]
         total = [jnp.zeros((3 * ch, 3 * ch), F32) for _ in range(3)]
         for xp in range(4):
-            steps = REACH[xp]
+            steps = reach(xp, 2)
             rows = [
                 dpad[xp - 1 - ox, :, (1 - oy) * LANES : (1 - oy) * LANES + width]
                 for ox in steps
                 for oy in (-1, 0, 1)
             ]
-            product = dot_nt(jnp.concatenate(rows, axis=0), held[xp])
+            product = dot_nt(jnp.concatenate(rows, axis=0), held[start + xp])
             for n, ox in enumerate(steps):
                 total[ox + 1] = total[ox + 1] + product[3 * ch * n : 3 * ch * (n + 1)]
         return [total[i // 3][(i % 3) * ch : (i % 3 + 1) * ch] for i in range(9)]
@@ -355,22 +403,38 @@
     sum_a = Reduce(pack_a, wire_a, in_a, part_a, mid_a, inx_a, full_a, sem_ra)
     sum_b = Reduce(pack_b, wire_b, in_b, part_b, mid_b, inx_b, full_b, sem_rb)
 
-    lifted = []
-    for a in range(2):
-        pieces = []
-        for y in range(ny):
-            j, b = y // 2, y % 2
-            row = (2 * a + b) * ch
-            pieces.append(up[row : row + ch, j * LANES : (j + 1) * LANES])
-        lifted.append((jnp.concatenate(pieces, axis=1) * plane_mask(a)).astype(BF16))
-    send_halo(0, lifted)
-    first = conv(0, lifted, s_lift, a1)
-    acts = []
+    lifted = lift(parents, own_mask)
+    send_edges(0, lifted, 0)
+    acc[...] = jnp.zeros(acc.shape, F32)
+    arrive(0, (3, 6))
+    low, high = tile(0, 3), tile(0, 6)
     for x in range(2):
-        pre1[x] = first[x]
-        acts.append((plane_mask(x) * first[x] * jax.nn.sigmoid(first[x])).astype(BF16))
-    send_halo(1, acts)
-    second = conv(1, acts, s_act, a2)
+        spread(s_lift, x + 2, lifted[x], low, high)
+        add(a1, s_lift, x + 2, 4)
+    arrive(4, (0, 1))
+    arrive(0, (0, 1, 2, 4, 5, 7))
+    around = []
+    for side in (0, 1):
+        around.append(mask_halo[side].astype(F32))
+        beside = lift(by_parity_of(grid_in[side]), around[side])
+        low, high = (tile(0, 4), tile(0, 7)) if side == 0 else (tile(0, 2), tile(0, 5))
+        for x in range(2):
+            xp = 4 * side + x
+            spread(s_lift, xp, beside[x], low, high)
+            add(a1, s_lift, xp, 4)
+    first = result(4)
+    rows = [mask_row(around[0], 1), plane_mask(0), plane_mask(1), mask_row(around[1], 0)]
+    acts = [(rows[x] * first[x] * jax.nn.sigmoid(first[x])).astype(BF16) for x in range(4)]
+    send_edges(1, acts, 0)
+    for x in range(2):
+        pre1[x] = first[x + 1]
+    acc[...] = jnp.zeros(acc.shape, F32)
+    arrive(1, (3, 6))
+    low, high = tile(1, 3), tile(1, 6)
+    for xp in range(4):
+        spread(s_act, xp, acts[xp], low, high)
+        add(a2, s_act, xp, 2)
+    second = result(2)
     deltas = []
     for x in range(2):
         v = second[x]
@@ -380,11 +444,13 @@
         slope = sig * (1.0 + v * (1.0 - sig))
         deltas.append((cot_plane(x) * m * slope).astype(BF16))
 
-    send_halo(2, deltas)
-    taps_two = tap_sums(deltas, s_act)
-    pack_taps(taps_two, pack_a)
     used = 14 * ch
-    pack_a[used:, :] = jnp.zeros((pack_a.shape[0] - used, LANES), F32)
+    for pack in (pack_a, pack_b):
+        if pack.shape[0] > used:
+            pack[used:, :] = jnp.zeros((pack.shape[0] - used, LANES), F32)
+    send_planes(2, deltas)
+    send_edges(2, deltas, 8)
+    pack_taps(tap_sums(deltas, s_act, 0), pack_a)
     sum_a.begin()
     back = conv(2, deltas, s_grad, b2)
     deltas = []
@@ -393,10 +459,14 @@
         sig = jax.nn.sigmoid(v)
         slope = sig * (1.0 + v * (1.0 - sig))
         deltas.append((back[x] * plane_mask(x) * slope).astype(BF16))
-    send_halo(3, deltas)
-    pack_taps(tap_sums(deltas, s_lift), pack_b)
+    send_planes(3, deltas)
+    send_edges(3, deltas, 8)
+    pack_taps(tap_sums(deltas, s_lift, 1), pack_b)
+    sum_b.begin()
     sum_a.second()
     back = conv(3, deltas, s_grad, b1)
+    sum_b.second()
+    sum_a.third()
     du = [(back[x] * plane_mask(x)).astype(BF16) for x in range(2)]
     stacked = jnp.concatenate(
         [
@@ -406,36 +476,73 @@
         ],
         axis=0,
     )
-    pack_b[used : used + 4 * ch, :] = dot_nt(stacked, parents)
-    rest = used + 4 * ch
-    if pack_b.shape[0] > rest:
-        pack_b[rest:, :] = jnp.zeros((pack_b.shape[0] - rest, LANES), F32)
-    sum_b.begin()
+    grad_up = dot_nt(stacked, parents)
+    part_c = pack_c.shape[1]
+    for d in range(pack_c.shape[0]):
+        if (d + 1) * part_c <= 4 * ch:
+            pack_c[d] = grad_up[d * part_c : (d + 1) * part_c]
+        else:
+            pack_c[d] = jnp.zeros((part_c, LANES), F32)
+
+    def scatter_copy(k):
+        to = lax.rem(me + k, n_dev)
+        return pltpu.make_async_remote_copy(
+            src_ref=pack_c.at[to],
+            dst_ref=in_c.at[k],
+            send_sem=sem_c.at[0, 0, k],
+            recv_sem=sem_c.at[0, 1, k],
+            device_id=(to // n_xy, lax.rem(to, n_xy)),
+            device_id_type=MESH,
+        )
+
+    def gather_copy(k):
+        to = lax.rem(me + k, n_dev)
+        return pltpu.make_async_remote_copy(
+            src_ref=full_c.at[me],
+            dst_ref=full_c.at[me],
+            send_sem=sem_c.at[1, 0, k],
+            recv_sem=sem_c.at[1, 1, k],
+            device_id=(to // n_xy, lax.rem(to, n_xy)),
+            device_id_type=MESH,
+        )
+
+    each_device(lambda k: scatter_copy(k).start())
+    in_c[0] = pack_c[me]
     by_parity = dot_tn(wup[...], stacked)
     kept = jnp.where(even, by_parity[:ch], by_parity[ch:])
     paired = kept + pltpu.roll(kept, half - 1, 1)
     parent_grad = jnp.where(even, paired, jnp.zeros_like(paired)).astype(BF16)
-    wide_grad = jnp.concatenate([parent_grad, jnp.zeros_like(parent_grad)], axis=0)
-    slot_grad[...] = dot_nt(hot, wide_grad).astype(BF16).reshape(slot_grad.shape)
+    compact = jnp.concatenate(
+        [dot_nt(parent_grad[:, h * 2 * LANES : (h + 1) * 2 * LANES], twice) for h in range(2)],
+        axis=1,
+    )
+    compact = jnp.concatenate([compact, jnp.zeros_like(compact)], axis=0).astype(BF16)
+    slot_grad[...] = dot_nt(hot, compact).astype(BF16).reshape(slot_grad.shape)
     each_device(lambda k: back_copy(k).start())
     ret[me] = slot_grad[0]
-    sum_a.third()
-    sum_b.second()
+    sum_b.third()
     sum_a.fourth()
-    sum_b.third()
+    each_device(lambda k: scatter_copy(k).wait())
+    total = in_c[0]
+    for d in range(1, n_dev):
+        total = total + in_c[d]
+    full_c[me] = total
+    each_device(lambda k: gather_copy(k).start())
+    sum_b.fourth()
     each_device(lambda k: back_copy(k).wait())
     returned = ret[...].reshape(slots, LANES).astype(F32).T[:ch]
     ret_out[...] = jnp.where(live, returned, 0.0).astype(BF16)
     out_a[...] = sum_a.done()
-    sum_b.fourth()
+    each_device(lambda k: gather_copy(k).wait())
+    out_c[...] = full_c[...].reshape(out_c.shape)
     out_b[...] = sum_b.done()
-    for e in range(4):
-        for side in range(8):
+    for e in range(5):
+        for side in USED[e]:
             there, copy = halo_copy(e, side)
             pl.when(there)(copy.wait_send)
 
 
-def finish_kernel(scale, dims, dec, ret, full_a, full_b, dec_out, ret_out, g1_out, g2_out, gup_out):
+def finish_kernel(scale, dims, dec, ret, full_a, full_b, full_c, dec_out, ret_out, g1_out, g2_out, gup_out):
     ch, ny = dims
     width = ny * LANES
     for x in range(2):
@@ -450,7 +557,7 @@
             pair = full[(9 + i // 2) * ch : (10 + i // 2) * ch].astype(F32) * scale
             out[3 * i + 2] = pair[:, :ch] if i % 2 == 0 else pair[:, ch:]
     for p in range(4):
-        tile = full_b[(14 + p) * ch : (15 + p) * ch].astype(F32) * scale
+        tile = full_c[p * ch : (p + 1) * ch] * scale
         gup_out[2 * p] = tile[:, :ch]
         gup_out[2 * p + 1] = tile[:, ch:]
 
@@ -467,7 +574,7 @@
     width = ny * size_z
     unit = n_dev * 16
     rows_a = -(-14 * ch // unit) * unit
-    rows_b = -(-18 * ch // unit) * unit
+    rows_c = -(-4 * ch // (8 * n_dev)) * 8 * n_dev
 
     def reduce_scratch(rows):
         per = rows // n_gz
@@ -485,16 +592,17 @@
     vmem = pl.BlockSpec(memory_space=pltpu.VMEM)
     most = max(n_gz, n_xy) - 1
     dma = pltpu.SemaphoreType.DMA
-    dec, ret, full_a, full_b = pl.pallas_call(
+    dec, ret, full_a, full_b, full_c = pl.pallas_call(
         functools.partial(all_kernel, (n_gz, n_xy, ch, ny)),
         out_shape=(
             jax.ShapeDtypeStruct((ch, voxels), BF16),
             jax.ShapeDtypeStruct((ch, slot_total), BF16),
             jax.ShapeDtypeStruct((rows_a, LANES), BF16),
-            jax.ShapeDtypeStruct((rows_b, LANES), BF16),
+            jax.ShapeDtypeStruct((rows_a, LANES), BF16),
+            jax.ShapeDtypeStruct((rows_c, LANES), F32),
         ),
         in_specs=[vmem] * 8,
-        out_specs=(vmem,) * 4,
+        out_specs=(vmem,) * 5,
         scratch_shapes=[
             pltpu.VMEM((n_dev, cap, LANES), BF16),
             pltpu.VMEM((4 * ch, 2 * ch), BF16),
@@ -505,23 +613,31 @@
             pltpu.VMEM((9 * ch, 3 * ch), BF16),
             pltpu.VMEM((9 * ch, 3 * ch), BF16),
             pltpu.VMEM((9 * ch, 3 * ch), BF16),
-            pltpu.VMEM((4, 2, ch, width), BF16),
-            pltpu.VMEM((4, 2, ch, width), BF16),
+            pltpu.VMEM((ch, 2 * LANES), BF16),
+            pltpu.VMEM((2, ch, 2 * LANES), BF16),
+            pltpu.VMEM((2 * ny, LANES), BF16),
+            pltpu.VMEM((2, 2 * ny, LANES), BF16),
+            pltpu.VMEM((2, 2, ch, width), BF16),
+            pltpu.VMEM((2, 2, ch, width), BF16),
             pltpu.VMEM((4, 2, ch, LANES), BF16),
             pltpu.VMEM((4, 6, ch, LANES), BF16),
+            pltpu.VMEM((6, 3 * ch, width), BF16),
             pltpu.VMEM((4, 3 * ch, width), BF16),
             pltpu.VMEM((4, 3 * ch, width), BF16),
-            pltpu.VMEM((4, 3 * ch, width), BF16),
-            pltpu.VMEM((2, ch, width + 2 * LANES), F32),
+            pltpu.VMEM((4, ch, width + 2 * LANES), F32),
             pltpu.VMEM((2, ch, width + 2 * LANES), BF16),
             pltpu.VMEM((2, ch, width), F32),
             *reduce_scratch(rows_a),
-            *reduce_scratch(rows_b),
+            *reduce_scratch(rows_a),
+            pltpu.VMEM((n_dev, rows_c // n_dev, LANES), F32),
+            pltpu.VMEM((n_dev, rows_c // n_dev, LANES), F32),
+            pltpu.VMEM((n_dev, rows_c // n_dev, LANES), F32),
             dma((2, n_dev)),
             dma((2, n_dev)),
-            dma((2, 4, 8)),
+            dma((2, 5, 8)),
             dma((2, 4, most)),
             dma((2, 4, most)),
+            dma((2, 2, n_dev)),
         ],
         compiler_params=pltpu.CompilerParams(
             collective_id=0, has_side_effects=True, vmem_limit_bytes=56 * 1024 * 1024
@@ -537,9 +653,9 @@
             jax.ShapeDtypeStruct((27, ch, ch), F32),
             jax.ShapeDtypeStruct((8, ch, ch), F32),
         ),
-        in_specs=[vmem] * 4,
+        in_specs=[vmem] * 5,
         out_specs=(vmem,) * 5,
-    )(dec, ret, full_a, full_b)
+    )(dec, ret, full_a, full_b, full_c)
 
 
 def solution(mesh):

time: 75.6 us -> 64.8 us (0.86)
  Pallas kernels: 74.4 us -> 63.8 us
    pallas_call x1, Pallas kernels: 71.6 us -> 60.9 us  [local(): pl.pallas_call(functools.partial(all_kernel, (n_gz, n_xy, ch, ny)), out_s...]
where the time goes in v3:
time: 64.8 us; the launch traced here: 64.4 us
  Pallas kernels  63.8 us (98%)
    pallas_call x1, Pallas kernels, local(): pl.pallas_call(functools.partial(all_kernel, (n_gz, n_xy, ch, ny)), out_s...  60.9 us
    pallas_call x1, Pallas kernels, local(): pl.pallas_call(functools.partial(finish_kernel, scale, (ch, ny)), out_sha...  2.85 us

profile of v3, /device:TPU:0, one launch (start us, length us, event | category | flops | bytes accessed | tf_op | source)
XLA Modules:
  0.0 64.4 jit_solution(11861472724232719448)
XLA Ops:
  0.6 60.9 %shard_map.119 = (bf16[64,2048]{1,0:T(8,128)(2,1)}, bf16[64,512]{1,0:T(8,128)(2,1)}, bf16[1024,128]{1,0:T(8,128)(2,1)}, bf16[1024,128]{1,0:T(8,128)(2,1)}, f32[256,128]{1,0:T(8,128)}) custom-call(bf16[1,64,512]{2,1,0:T(8,128)(2,1)} %feat.1, s32[1,512]{1,0:T(1,128)} %cell.1, s32[1,32]{1,0:T(1,128)} %count.1, bf16[8,64,64]{2,1,0:T(8,128)(2,1)} %w_up.1, ...), custom_call_target="tpu_custom_call" | custom-call | tf_op jit(solution)/shard_map/pallas_call | solution.py:595
  61.6 2.9 %shard_map.120 = (bf16[64,2,8,128]{3,2,1,0:T(8,128)(2,1)}, bf16[1,64,512]{2,1,0:T(8,128)(2,1)}, f32[27,64,64]{2,1,0:T(8,128)}, f32[27,64,64]{2,1,0:T(8,128)}, f32[8,64,64]{2,1,0:T(8,128)}) custom-call(bf16[64,2048]{1,0:T(8,128)(2,1)} %get-tuple-element.10.dec, bf16[64,512]{1,0:T(8,128)(2,1)} %get-tuple-element.11.ret, ...), custom_call_target="tpu_custom_call" | custom-call | tf_op jit(solution)/shard_map/pallas_call | solution.py:647

commit v4 on v3

--- a/solution.py
+++ b/solution.py
@@ -39,7 +39,7 @@
     s_lift, s_act, s_grad, acc, dpad, pre1,
     pack_a, wire_a, in_a, part_a, mid_a, inx_a, full_a,
     pack_b, wire_b, in_b, part_b, mid_b, inx_b, full_b,
-    pack_c, in_c, full_c,
+    full_c,
     sem_to, sem_back, sem_halo, sem_ra, sem_rb, sem_c,
 ):
     n_gz, n_xy, ch, ny = dims
@@ -60,14 +60,23 @@
 
     lax.fori_loop(1, n_dev, greet, 0)
 
-    def weights(i, carry):
-        rows = pl.ds(pl.multiple_of(i * ch, ch), ch)
-        for w, a, b in ((w1, a1, b1), (w2, a2, b2)):
-            a[rows, :] = jnp.concatenate([w[3 * i + t] for t in range(3)], axis=1)
-            b[rows, :] = jnp.concatenate(
+    def stack_forward(w, into):
+        def step(i, carry):
+            rows = pl.ds(pl.multiple_of(i * ch, ch), ch)
+            into[rows, :] = jnp.concatenate([w[3 * i + t] for t in range(3)], axis=1)
+            return carry
+
+        lax.fori_loop(0, 9, step, 0)
+
+    def stack_backward(w, into):
+        def step(i, carry):
+            rows = pl.ds(pl.multiple_of(i * ch, ch), ch)
+            into[rows, :] = jnp.concatenate(
                 [w[26 - 3 * i - t].astype(F32).T.astype(BF16) for t in range(3)], axis=1
             )
-        return carry
+            return carry
+
+        lax.fori_loop(0, 9, step, 0)
 
     def near(dx, dz):
         x, z = xy + dx, gz + dz
@@ -129,29 +138,31 @@
     for i in range(4):
         wup[i * ch : (i + 1) * ch, :] = jnp.concatenate([w_up[2 * i], w_up[2 * i + 1]], axis=1)
     mask_out[...] = jnp.concatenate([mask_in[0], mask_in[1]], axis=0).astype(F32).astype(BF16)
+    stack_forward(w1, a1)
     pl.semaphore_wait(barrier, n_dev - 1)
 
-    def to_copy(k):
-        to = lax.rem(me + k, n_dev)
-        return pltpu.make_async_remote_copy(
-            src_ref=src.at[to],
-            dst_ref=got.at[k],
-            send_sem=sem_to.at[0, k],
-            recv_sem=sem_to.at[1, k],
-            device_id=(to // n_xy, lax.rem(to, n_xy)),
-            device_id_type=MESH,
-        )
-
-    def back_copy(k):
-        to = lax.rem(me + n_dev - k, n_dev)
-        return pltpu.make_async_remote_copy(
-            src_ref=slot_grad.at[k],
-            dst_ref=ret.at[me],
-            send_sem=sem_back.at[0, k],
-            recv_sem=sem_back.at[1, k],
-            device_id=(to // n_xy, lax.rem(to, n_xy)),
-            device_id_type=MESH,
-        )
+    def exchange(source, landed, sems):
+        def copy(k):
+            to = lax.rem(me + k, n_dev)
+            return pltpu.make_async_remote_copy(
+                src_ref=source(to),
+                dst_ref=landed.at[me],
+                send_sem=sems.at[0],
+                recv_sem=sems.at[1],
+                device_id=(to // n_xy, lax.rem(to, n_xy)),
+                device_id_type=MESH,
+            )
+
+        def finish():
+            others = landed.at[pl.ds(0, n_dev - 1)]
+            pltpu.make_async_copy(others, others, sems.at[0]).wait()
+            pltpu.make_async_copy(others, others, sems.at[1]).wait()
+
+        return copy, finish
+
+    to_copy, to_finish = exchange(lambda to: src.at[to], got, sem_to)
+    back_copy, back_finish = exchange(lambda to: slot_grad.at[to], ret, sem_back)
+    gather_copy, gather_finish = exchange(lambda to: full_c.at[me], full_c, sem_c)
 
     def each_device(action):
         def step(k, carry):
@@ -164,9 +175,9 @@
     for side in USED[4]:
         there, copy = halo_copy(4, side)
         pl.when(there)(copy.start)
-    got[0] = src[me]
-    lax.fori_loop(0, 9, weights, 0)
-    each_device(lambda k: to_copy(k).wait())
+    got[me] = src[me]
+    stack_forward(w2, a2)
+    to_finish()
 
     listed = got[...].reshape(slots, LANES)
     half = 4 * LANES
@@ -288,7 +299,7 @@
     def result(count):
         return [acc[x, :, LANES : LANES + width] for x in range(count)]
 
-    def conv(e, fields, held, matrix):
+    def conv(e, fields, held, matrix, meanwhile=()):
         acc[...] = jnp.zeros(acc.shape, F32)
         arrive(e, (3, 6))
         low, high = tile(e, 3), tile(e, 6)
@@ -296,6 +307,8 @@
             spread(held, xp, fields[xp - 1], low, high)
             add(matrix, held, xp, 2)
         arrive(e, (0, 1, 2, 4, 5, 7))
+        for action in meanwhile:
+            action()
         spread(held, 0, plane_in[e - 2, 0], tile(e, 4), tile(e, 7))
         add(matrix, held, 0, 2)
         spread(held, 3, plane_in[e - 2, 1], tile(e, 2), tile(e, 5))
@@ -405,6 +418,7 @@
 
     lifted = lift(parents, own_mask)
     send_edges(0, lifted, 0)
+    stack_backward(w2, b2)
     acc[...] = jnp.zeros(acc.shape, F32)
     arrive(0, (3, 6))
     low, high = tile(0, 3), tile(0, 6)
@@ -426,6 +440,7 @@
     rows = [mask_row(around[0], 1), plane_mask(0), plane_mask(1), mask_row(around[1], 0)]
     acts = [(rows[x] * first[x] * jax.nn.sigmoid(first[x])).astype(BF16) for x in range(4)]
     send_edges(1, acts, 0)
+    stack_backward(w1, b1)
     for x in range(2):
         pre1[x] = first[x + 1]
     acc[...] = jnp.zeros(acc.shape, F32)
@@ -464,9 +479,7 @@
     pack_taps(tap_sums(deltas, s_lift, 1), pack_b)
     sum_b.begin()
     sum_a.second()
-    back = conv(3, deltas, s_grad, b1)
-    sum_b.second()
-    sum_a.third()
+    back = conv(3, deltas, s_grad, b1, (sum_b.second, sum_a.third))
     du = [(back[x] * plane_mask(x)).astype(BF16) for x in range(2)]
     stacked = jnp.concatenate(
         [
@@ -477,37 +490,6 @@
         axis=0,
     )
     grad_up = dot_nt(stacked, parents)
-    part_c = pack_c.shape[1]
-    for d in range(pack_c.shape[0]):
-        if (d + 1) * part_c <= 4 * ch:
-            pack_c[d] = grad_up[d * part_c : (d + 1) * part_c]
-        else:
-            pack_c[d] = jnp.zeros((part_c, LANES), F32)
-
-    def scatter_copy(k):
-        to = lax.rem(me + k, n_dev)
-        return pltpu.make_async_remote_copy(
-            src_ref=pack_c.at[to],
-            dst_ref=in_c.at[k],
-            send_sem=sem_c.at[0, 0, k],
-            recv_sem=sem_c.at[0, 1, k],
-            device_id=(to // n_xy, lax.rem(to, n_xy)),
-            device_id_type=MESH,
-        )
-
-    def gather_copy(k):
-        to = lax.rem(me + k, n_dev)
-        return pltpu.make_async_remote_copy(
-            src_ref=full_c.at[me],
-            dst_ref=full_c.at[me],
-            send_sem=sem_c.at[1, 0, k],
-            recv_sem=sem_c.at[1, 1, k],
-            device_id=(to // n_xy, lax.rem(to, n_xy)),
-            device_id_type=MESH,
-        )
-
-    each_device(lambda k: scatter_copy(k).start())
-    in_c[0] = pack_c[me]
     by_parity = dot_tn(wup[...], stacked)
     kept = jnp.where(even, by_parity[:ch], by_parity[ch:])
     paired = kept + pltpu.roll(kept, half - 1, 1)
@@ -517,23 +499,26 @@
         axis=1,
     )
     compact = jnp.concatenate([compact, jnp.zeros_like(compact)], axis=0).astype(BF16)
-    slot_grad[...] = dot_nt(hot, compact).astype(BF16).reshape(slot_grad.shape)
+    terms = jnp.concatenate([grad_up[:, :ch], grad_up[:, ch:]], axis=0)
+    if slots > 8 * ch:
+        terms = jnp.concatenate([terms, jnp.zeros((slots - 8 * ch, ch), F32)], axis=0)
+    both = jnp.concatenate([dot_nt(hot, compact)[:, :ch], terms], axis=1)
+    slot_grad[...] = both.astype(BF16).reshape(slot_grad.shape)
     each_device(lambda k: back_copy(k).start())
-    ret[me] = slot_grad[0]
+    ret[me] = slot_grad[me]
     sum_b.third()
     sum_a.fourth()
-    each_device(lambda k: scatter_copy(k).wait())
-    total = in_c[0]
+    back_finish()
+    total = ret[0].astype(F32)
     for d in range(1, n_dev):
-        total = total + in_c[d]
-    full_c[me] = total
+        total = total + ret[d].astype(F32)
+    full_c[me] = total.astype(BF16)
     each_device(lambda k: gather_copy(k).start())
     sum_b.fourth()
-    each_device(lambda k: back_copy(k).wait())
     returned = ret[...].reshape(slots, LANES).astype(F32).T[:ch]
     ret_out[...] = jnp.where(live, returned, 0.0).astype(BF16)
     out_a[...] = sum_a.done()
-    each_device(lambda k: gather_copy(k).wait())
+    gather_finish()
     out_c[...] = full_c[...].reshape(out_c.shape)
     out_b[...] = sum_b.done()
     for e in range(5):
@@ -557,9 +542,9 @@
             pair = full[(9 + i // 2) * ch : (10 + i // 2) * ch].astype(F32) * scale
             out[3 * i + 2] = pair[:, :ch] if i % 2 == 0 else pair[:, ch:]
     for p in range(4):
-        tile = full_c[p * ch : (p + 1) * ch] * scale
-        gup_out[2 * p] = tile[:, :ch]
-        gup_out[2 * p + 1] = tile[:, ch:]
+        for e in range(2):
+            row = (4 * e + p) * ch
+            gup_out[2 * p + e] = full_c[row : row + ch].astype(F32)[:, ch:] * scale
 
 
 def local(
@@ -574,7 +559,7 @@
     width = ny * size_z
     unit = n_dev * 16
     rows_a = -(-14 * ch // unit) * unit
-    rows_c = -(-4 * ch // (8 * n_dev)) * 8 * n_dev
+    assert 8 * ch <= slot_total
 
     def reduce_scratch(rows):
         per = rows // n_gz
@@ -599,7 +584,7 @@
             jax.ShapeDtypeStruct((ch, slot_total), BF16),
             jax.ShapeDtypeStruct((rows_a, LANES), BF16),
             jax.ShapeDtypeStruct((rows_a, LANES), BF16),
-            jax.ShapeDtypeStruct((rows_c, LANES), F32),
+            jax.ShapeDtypeStruct((slot_total, LANES), BF16),
         ),
         in_specs=[vmem] * 8,
         out_specs=(vmem,) * 5,
@@ -629,15 +614,13 @@
             pltpu.VMEM((2, ch, width), F32),
             *reduce_scratch(rows_a),
             *reduce_scratch(rows_a),
-            pltpu.VMEM((n_dev, rows_c // n_dev, LANES), F32),
-            pltpu.VMEM((n_dev, rows_c // n_dev, LANES), F32),
-            pltpu.VMEM((n_dev, rows_c // n_dev, LANES), F32),
-            dma((2, n_dev)),
-            dma((2, n_dev)),
+            pltpu.VMEM((n_dev, cap, LANES), BF16),
+            dma((2,)),
+            dma((2,)),
             dma((2, 5, 8)),
             dma((2, 4, most)),
             dma((2, 4, most)),
-            dma((2, 2, n_dev)),
+            dma((2,)),
         ],
         compiler_params=pltpu.CompilerParams(
             collective_id=0, has_side_effects=True, vmem_limit_bytes=56 * 1024 * 1024

time: 64.8 us -> 60.9 us (0.940)
  Pallas kernels: 63.8 us -> 60 us
    pallas_call x1, Pallas kernels: 60.9 us -> 57.2 us  [local(): pl.pallas_call(functools.partial(all_kernel, (n_gz, n_xy, ch, ny)), out_s...]
where the time goes in v4:
time: 60.9 us; the launch traced here: 60.7 us
  Pallas kernels  60 us (99%)
  between operations  0.64 us (1%)
    pallas_call x1, Pallas kernels, local(): pl.pallas_call(functools.partial(all_kernel, (n_gz, n_xy, ch, ny)), out_s...  57.2 us
    pallas_call x1, Pallas kernels, local(): pl.pallas_call(functools.partial(finish_kernel, scale, (ch, ny)), out_sha...  2.87 us

profile of v4, /device:TPU:0, one launch (start us, length us, event | category | flops | bytes accessed | tf_op | source)
XLA Modules:
  0.0 60.7 jit_solution(16300544315193254186)
XLA Ops:
  0.6 57.2 %shard_map.119 = (bf16[64,2048]{1,0:T(8,128)(2,1)}, bf16[64,512]{1,0:T(8,128)(2,1)}, bf16[1024,128]{1,0:T(8,128)(2,1)}, bf16[1024,128]{1,0:T(8,128)(2,1)}, bf16[512,128]{1,0:T(8,128)(2,1)}) custom-call(bf16[1,64,512]{2,1,0:T(8,128)(2,1)} %feat.1, s32[1,512]{1,0:T(1,128)} %cell.1, s32[1,32]{1,0:T(1,128)} %count.1, bf16[8,64,64]{2,1,0:T(8,128)(2,1)} %w_up.1, ...), custom_call_target="tpu_custom_call" | custom-call | tf_op jit(solution)/shard_map/pallas_call | solution.py:580
  57.8 2.9 %shard_map.120 = (bf16[64,2,8,128]{3,2,1,0:T(8,128)(2,1)}, bf16[1,64,512]{2,1,0:T(8,128)(2,1)}, f32[27,64,64]{2,1,0:T(8,128)}, f32[27,64,64]{2,1,0:T(8,128)}, f32[8,64,64]{2,1,0:T(8,128)}) custom-call(bf16[64,2048]{1,0:T(8,128)(2,1)} %get-tuple-element.10.dec, bf16[64,512]{1,0:T(8,128)(2,1)} %get-tuple-element.11.ret, ...), custom_call_target="tpu_custom_call" | custom-call | tf_op jit(solution)/shard_map/pallas_call | solution.py:630

commit v5 on v4

--- a/solution.py
+++ b/solution.py
@@ -30,8 +30,9 @@
 
 def all_kernel(
     dims,
-    feat, cell, count, w_up, w1, w2, mask_in, cot_in,
+    feat, cell, count, w_up, w1_in, w2_in, mask_in, cot_hbm,
     dec, ret_out, out_a, out_b, out_c,
+    w1, w2, cot_in, sem_in,
     src, wup, got, slot_grad, ret,
     a1, b1, a2, b2,
     grid, grid_in, mask_out, mask_halo,
@@ -54,10 +55,16 @@
     def greet(k, carry):
         to = lax.rem(me + k, n_dev)
         pl.semaphore_signal(
-            barrier, inc=1, device_id=(to // n_xy, lax.rem(to, n_xy)), device_id_type=MESH
+            barrier, inc=1, device_id=(lax.div(to, n_xy), lax.rem(to, n_xy)), device_id_type=MESH
         )
         return carry
 
+    loads = [
+        pltpu.make_async_copy(source, into, sem_in.at[n])
+        for n, (source, into) in enumerate(((w1_in, w1), (w2_in, w2), (cot_hbm, cot_in)))
+    ]
+    for load in loads:
+        load.start()
     lax.fori_loop(1, n_dev, greet, 0)
 
     def stack_forward(w, into):
@@ -138,6 +145,7 @@
     for i in range(4):
         wup[i * ch : (i + 1) * ch, :] = jnp.concatenate([w_up[2 * i], w_up[2 * i + 1]], axis=1)
     mask_out[...] = jnp.concatenate([mask_in[0], mask_in[1]], axis=0).astype(F32).astype(BF16)
+    loads[0].wait()
     stack_forward(w1, a1)
     pl.semaphore_wait(barrier, n_dev - 1)
 
@@ -149,7 +157,7 @@
                 dst_ref=landed.at[me],
                 send_sem=sems.at[0],
                 recv_sem=sems.at[1],
-                device_id=(to // n_xy, lax.rem(to, n_xy)),
+                device_id=(lax.div(to, n_xy), lax.rem(to, n_xy)),
                 device_id_type=MESH,
             )
 
@@ -176,7 +184,9 @@
         there, copy = halo_copy(4, side)
         pl.when(there)(copy.start)
     got[me] = src[me]
+    loads[1].wait()
     stack_forward(w2, a2)
+    loads[2].wait()
     to_finish()
 
     listed = got[...].reshape(slots, LANES)
@@ -467,7 +477,7 @@
     send_edges(2, deltas, 8)
     pack_taps(tap_sums(deltas, s_act, 0), pack_a)
     sum_a.begin()
-    back = conv(2, deltas, s_grad, b2)
+    back = conv(2, deltas, s_grad, b2, (sum_a.second,))
     deltas = []
     for x in range(2):
         v = pre1[x]
@@ -478,8 +488,8 @@
     send_edges(3, deltas, 8)
     pack_taps(tap_sums(deltas, s_lift, 1), pack_b)
     sum_b.begin()
-    sum_a.second()
-    back = conv(3, deltas, s_grad, b1, (sum_b.second, sum_a.third))
+    sum_a.third()
+    back = conv(3, deltas, s_grad, b1, (sum_b.second, sum_a.fourth))
     du = [(back[x] * plane_mask(x)).astype(BF16) for x in range(2)]
     stacked = jnp.concatenate(
         [
@@ -507,14 +517,13 @@
     each_device(lambda k: back_copy(k).start())
     ret[me] = slot_grad[me]
     sum_b.third()
-    sum_a.fourth()
     back_finish()
+    sum_b.fourth()
     total = ret[0].astype(F32)
     for d in range(1, n_dev):
         total = total + ret[d].astype(F32)
     full_c[me] = total.astype(BF16)
     each_device(lambda k: gather_copy(k).start())
-    sum_b.fourth()
     returned = ret[...].reshape(slots, LANES).astype(F32).T[:ch]
     ret_out[...] = jnp.where(live, returned, 0.0).astype(BF16)
     out_a[...] = sum_a.done()
@@ -586,9 +595,13 @@
             jax.ShapeDtypeStruct((rows_a, LANES), BF16),
             jax.ShapeDtypeStruct((slot_total, LANES), BF16),
         ),
-        in_specs=[vmem] * 8,
+        in_specs=[vmem] * 4 + [pl.BlockSpec(memory_space=pl.ANY)] * 2 + [vmem, pl.BlockSpec(memory_space=pl.ANY)],
         out_specs=(vmem,) * 5,
         scratch_shapes=[
+            pltpu.VMEM(conv_one.shape, BF16),
+            pltpu.VMEM(conv_two.shape, BF16),
+            pltpu.VMEM(cotangent.shape, BF16),
+            dma((3,)),
             pltpu.VMEM((n_dev, cap, LANES), BF16),
             pltpu.VMEM((4 * ch, 2 * ch), BF16),
             pltpu.VMEM((n_dev, cap, LANES), BF16),

time: 60.9 us -> 61.3 us (level)
  no operation moved by 1% of the time
where the time goes in v5:
time: 61.3 us; the launch traced here: 61.1 us
  Pallas kernels  60.5 us (99%)
  between operations  0.64 us (1%)
    pallas_call x1, Pallas kernels, local(): pl.pallas_call(functools.partial(all_kernel, (n_gz, n_xy, ch, ny)), out_s...  57.6 us
    pallas_call x1, Pallas kernels, local(): pl.pallas_call(functools.partial(finish_kernel, scale, (ch, ny)), out_sha...  2.87 us

profile of v5, /device:TPU:0, one launch (start us, length us, event | category | flops | bytes accessed | tf_op | source)
XLA Modules:
  0.0 61.1 jit_solution(13944945882840601617)
XLA Ops:
  0.6 57.6 %shard_map.119 = (bf16[64,2048]{1,0:T(8,128)(2,1)}, bf16[64,512]{1,0:T(8,128)(2,1)}, bf16[1024,128]{1,0:T(8,128)(2,1)}, bf16[1024,128]{1,0:T(8,128)(2,1)}, bf16[512,128]{1,0:T(8,128)(2,1)}) custom-call(bf16[1,64,512]{2,1,0:T(8,128)(2,1)} %feat.1, s32[1,512]{1,0:T(1,128)} %cell.1, s32[1,32]{1,0:T(1,128)} %count.1, bf16[8,64,64]{2,1,0:T(8,128)(2,1)} %w_up.1, ...), custom_call_target="tpu_custom_call" | custom-call | tf_op jit(solution)/shard_map/pallas_call | solution.py:589
  58.3 2.9 %shard_map.120 = (bf16[64,2,8,128]{3,2,1,0:T(8,128)(2,1)}, bf16[1,64,512]{2,1,0:T(8,128)(2,1)}, f32[27,64,64]{2,1,0:T(8,128)}, f32[27,64,64]{2,1,0:T(8,128)}, f32[8,64,64]{2,1,0:T(8,128)}) custom-call(bf16[64,2048]{1,0:T(8,128)(2,1)} %get-tuple-element.10.dec, bf16[64,512]{1,0:T(8,128)(2,1)} %get-tuple-element.11.ret, ...), custom_call_target="tpu_custom_call" | custom-call | tf_op jit(solution)/shard_map/pallas_call | solution.py:643

commit v6 on v5

--- a/solution.py
+++ b/solution.py
@@ -316,11 +316,12 @@
         for xp in (1, 2):
             spread(held, xp, fields[xp - 1], low, high)
             add(matrix, held, xp, 2)
-        arrive(e, (0, 1, 2, 4, 5, 7))
+        arrive(e, (0, 4, 7))
+        spread(held, 0, plane_in[e - 2, 0], tile(e, 4), tile(e, 7))
+        add(matrix, held, 0, 2)
         for action in meanwhile:
             action()
-        spread(held, 0, plane_in[e - 2, 0], tile(e, 4), tile(e, 7))
-        add(matrix, held, 0, 2)
+        arrive(e, (1, 2, 5))
         spread(held, 3, plane_in[e - 2, 1], tile(e, 2), tile(e, 5))
         add(matrix, held, 3, 2)
         return result(2)
@@ -435,10 +436,10 @@
     for x in range(2):
         spread(s_lift, x + 2, lifted[x], low, high)
         add(a1, s_lift, x + 2, 4)
-    arrive(4, (0, 1))
-    arrive(0, (0, 1, 2, 4, 5, 7))
     around = []
     for side in (0, 1):
+        arrive(4, (side,))
+        arrive(0, (0, 4, 7) if side == 0 else (1, 2, 5))
         around.append(mask_halo[side].astype(F32))
         beside = lift(by_parity_of(grid_in[side]), around[side])
         low, high = (tile(0, 4), tile(0, 7)) if side == 0 else (tile(0, 2), tile(0, 5))

time: 61.3 us -> 61.1 us (level)
  no operation moved by 1% of the time
where the time goes in v6:
time: 61.1 us; the launch traced here: 60.9 us
  Pallas kernels  60.3 us (99%)
  between operations  0.64 us (1%)
    pallas_call x1, Pallas kernels, local(): pl.pallas_call(functools.partial(all_kernel, (n_gz, n_xy, ch, ny)), out_s...  57.4 us
    pallas_call x1, Pallas kernels, local(): pl.pallas_call(functools.partial(finish_kernel, scale, (ch, ny)), out_sha...  2.87 us

profile of v6, /device:TPU:0, one launch (start us, length us, event | category | flops | bytes accessed | tf_op | source)
XLA Modules:
  0.0 60.9 jit_solution(11379777195219273502)
XLA Ops:
  0.6 57.4 %shard_map.119 = (bf16[64,2048]{1,0:T(8,128)(2,1)}, bf16[64,512]{1,0:T(8,128)(2,1)}, bf16[1024,128]{1,0:T(8,128)(2,1)}, bf16[1024,128]{1,0:T(8,128)(2,1)}, bf16[512,128]{1,0:T(8,128)(2,1)}) custom-call(bf16[1,64,512]{2,1,0:T(8,128)(2,1)} %feat.1, s32[1,512]{1,0:T(1,128)} %cell.1, s32[1,32]{1,0:T(1,128)} %count.1, bf16[8,64,64]{2,1,0:T(8,128)(2,1)} %w_up.1, ...), custom_call_target="tpu_custom_call" | custom-call | tf_op jit(solution)/shard_map/pallas_call | solution.py:590
  58.0 2.9 %shard_map.120 = (bf16[64,2,8,128]{3,2,1,0:T(8,128)(2,1)}, bf16[1,64,512]{2,1,0:T(8,128)(2,1)}, f32[27,64,64]{2,1,0:T(8,128)}, f32[27,64,64]{2,1,0:T(8,128)}, f32[8,64,64]{2,1,0:T(8,128)}) custom-call(bf16[64,2048]{1,0:T(8,128)(2,1)} %get-tuple-element.10.dec, bf16[64,512]{1,0:T(8,128)(2,1)} %get-tuple-element.11.ret, ...), custom_call_target="tpu_custom_call" | custom-call | tf_op jit(solution)/shard_map/pallas_call | solution.py:644
